TPU v7x, 32 devices: a whole 2x2x4 slice. The times are simulated.
32 devices in a mesh: tm: 4 (over y, x), rows: 8 (over z, core).
Axes of the slice: x: 2, y: 2, z: 4, core: 2. Of those that a mesh axis runs over, the one named last changes fastest.
Arguments:
- frames: bfloat16 [8, 128, 128, 512], P('tm', 'rows'), may hold values from -6 to 6
- space_weight: bfloat16 [3, 3, 512, 512], replicated, may hold values from -0.09375 to 0.09375
- time_weight: bfloat16 [3, 512, 2, 256], replicated, may hold values from -0.15625 to 0.15625
- out_weight: bfloat16 [3, 3, 256, 256], replicated, may hold values from -0.125 to 0.125
Outputs:
- decoded: bfloat16 [16, 128, 128, 256], P('tm', 'rows')
All inputs are finite; a program needn't handle non-finite values.
Results may differ from a plain program's by a relative error of at most 0.0095.
Values may be sent and summed in bfloat16 or wider, within the bound.
No kernel may reach another device: no remote copies, remote signals or barrier semaphores. Data moves between devices by JAX's collectives and lax.ppermute only.
A program may use at most 128 MiB of HBM per device.

v0:
```python
import functools

import jax
import jax.numpy as jnp
from jax import lax
from jax.experimental import pallas as pl
from jax.experimental.pallas import tpu as pltpu
from jax.sharding import PartitionSpec as P

MIB = 1024 * 1024


def silu(v):
    half = 0.5 * v
    return half + half * jnp.tanh(half)


def activate(x_ref, act_ref, row, frame):
    width, channels = x_ref.shape[2:]
    step = 256
    column = lax.broadcasted_iota(jnp.int32, (width, step), 0)
    for start in range(0, channels, step):
        v = x_ref[row, frame, :, start : start + step].astype(jnp.float32)
        a = silu(v)
        before = jnp.where(column == 0, 0.0, pltpu.roll(a, 1, 0))
        after = jnp.where(column == width - 1, 0.0, pltpu.roll(a, width - 1, 0))
        for tap, value in enumerate((before, a, after)):
            act_ref[row, frame, :, tap * channels + start : tap * channels + start + step] = value.astype(
                jnp.bfloat16
            )


def convolve(x_ref, act_ref, w_ref, out_ref, source, target, group, between):
    _, frames, width, channels = x_ref.shape
    size = group * frames * width
    total = x_ref[pl.ds(source + 1, group)].reshape(size, channels).astype(jnp.float32)
    for tap in range(3):
        between(tap)
        lhs = act_ref[pl.ds(source + tap, group)].reshape(size, 3 * channels)
        total += jnp.dot(lhs, w_ref[tap], preferred_element_type=jnp.float32)
    out_ref[pl.ds(target, group)] = total.astype(jnp.bfloat16).reshape(group, frames, width, channels)


def lift(own_ref, before_ref, time_ref, x_ref, source, target, count):
    _, frames, width, channels = own_ref.shape
    depth = x_ref.shape[3]
    size = count * width
    window = [
        ref[pl.ds(source, count), frame].reshape(size, channels)
        for ref in (before_ref, own_ref)
        for frame in range(frames)
    ]
    for frame in range(frames):
        total = None
        for tap in range(3):
            part = jnp.dot(window[frame + tap], time_ref[tap], preferred_element_type=jnp.float32)
            total = part if total is None else total + part
        total = total.astype(jnp.bfloat16)
        for half in range(2):
            x_ref[pl.ds(target, count), 2 * frame + half] = total[:, half * depth : (half + 1) * depth].reshape(
                count, width, depth
            )


def stage_kernel(plan, *refs):
    refs = list(refs)
    sources = [refs.pop(0) for _ in range(plan["sources"])]
    w_ref = refs.pop(0)
    time_ref = refs.pop(0) if plan["lifts"] else None
    for _ in range(plan["unread"]):
        refs.pop(0)
    outs = [refs.pop(0) for _ in range(plan["outs"])]
    x_ref, act_ref = [refs.pop(0) for _ in range(2)]
    frames = x_ref.shape[1]

    fetched = plan["fetched"]
    if fetched:
        in_sem = refs.pop(0)
        for source, start, count, target in plan["loads"]:
            for row in range(count):
                for frame in range(frames):
                    pltpu.make_async_copy(
                        sources[source].at[frame, start + row], x_ref.at[target + row, frame], in_sem.at[target + row]
                    ).start()
    weights = []
    if plan["fetch"]:
        w_hbm = w_ref
        w_ref, w_sem = [refs.pop(0) for _ in range(2)]
        weights = [pltpu.make_async_copy(w_hbm.at[tap], w_ref.at[tap], w_sem.at[tap]) for tap in range(3)]
    edges = []
    if plan["edges"]:
        edge_sem = refs.pop(0)
        edges = [
            pltpu.make_async_copy(
                sources[0].at[:, pl.ds(row, 1)], outs[plan["outs"] - len(plan["edges"]) + number], edge_sem.at[number]
            )
            for number, row in enumerate(plan["edges"])
        ]
    for copy in weights + edges:
        copy.start()
    if plan["staged"]:
        stage_ref, out_sem = [refs.pop(0) for _ in range(2)]

    for own, before, start, count, target in plan["lifts"]:
        step = min(count, 2)

        def body(number, carry, own=own, before=before, start=start, target=target, step=step):
            lift(
                sources[own], sources[before], time_ref, x_ref, start + number * step, target + number * step, step
            )
            return carry

        lax.fori_loop(0, count // step, body, 0)
    if not fetched:
        for source, start, count, target in plan["loads"]:
            x_ref[pl.ds(target, count)] = sources[source][pl.ds(start, count)]
    for out, row, count in plan["keeps"]:
        outs[out][...] = x_ref[pl.ds(row, count)]

    def prepare(row, frame):
        if fetched and frame == 0:
            pltpu.make_async_copy(x_ref.at[row], x_ref.at[row], in_sem.at[row]).wait()
        activate(x_ref, act_ref, row, frame)

    target = 0
    for number, (source, count, active, out, start) in enumerate(plan["runs"]):
        group = min(count, 2)
        steps = count // group

        def first(row, carry, source=source):
            for frame in range(frames):
                prepare(source + row, frame)
            return carry

        lax.fori_loop(active, group + 2, first, 0)

        def body(step, carry, last, source=source, target=target, group=group, out=out, start=start):
            def between(tap):
                if weights and number == 0 and last:
                    weights[tap].wait()
                if last:
                    return
                for at, (row, frame) in enumerate((r, f) for r in range(group) for f in range(frames)):
                    if at * 3 // (group * frames) == tap:
                        prepare(source + (step + 1) * group + 2 + row, frame)

            row = target + step * group if plan["staged"] else start + step * group
            to_ref = stage_ref if plan["staged"] else outs[out]
            convolve(x_ref, act_ref, w_ref, to_ref, source + step * group, row, group, between)
            if plan["staged"]:
                for frame in range(frames):
                    pltpu.make_async_copy(
                        stage_ref.at[pl.ds(row, group), frame],
                        outs[out].at[frame, pl.ds(start + step * group, group)],
                        out_sem.at[0],
                    ).start()
            return carry

        if steps > 1:
            lax.fori_loop(0, steps - 1, functools.partial(body, last=False), 0)
        body(steps - 1, 0, last=True)
        target += count

    if plan["staged"]:
        pltpu.make_async_copy(stage_ref, stage_ref, out_sem.at[0]).wait()
    for copy in edges:
        copy.wait()


def stage(
    name,
    sources,
    weight,
    loads,
    runs,
    out_shapes,
    dims,
    fetched=False,
    staged=False,
    lifts=(),
    time=None,
    keeps=(),
    into=None,
    after=(),
    edges=(),
    fetch=False,
):
    frames, width, channels = dims
    rows_in = max(target + count for *_, count, target in list(loads) + list(lifts))
    rows_out = sum(run[1] for run in runs)
    args = list(sources) + [weight]
    spaces = [pl.ANY if fetched else pltpu.VMEM] * len(sources) + [pltpu.HBM if fetch else pltpu.VMEM]
    if lifts:
        args.append(time)
        spaces.append(pltpu.VMEM)
    unread = list(after) + ([] if into is None else [into])
    args += unread
    spaces += [pl.ANY] * len(unread)
    out_spaces = [pltpu.HBM if staged else pltpu.VMEM] + [pltpu.VMEM] * (len(out_shapes) - 1 + len(edges))
    out_shapes = list(out_shapes) + [(frames, 1, width, channels)] * len(edges)
    plan = dict(
        sources=len(sources),
        unread=len(unread),
        outs=len(out_shapes),
        loads=loads,
        fetched=fetched,
        staged=staged,
        lifts=lifts,
        keeps=keeps,
        runs=runs,
        edges=edges,
        fetch=fetch,
    )
    scratch = [
        pltpu.VMEM((rows_in, frames, width, channels), jnp.bfloat16),
        pltpu.VMEM((rows_in, frames, width, 3 * channels), jnp.bfloat16),
    ]
    held = 2 * frames * width * channels * 4 * rows_in
    flops = 2 * rows_out * frames * width * 9 * channels * channels
    if lifts:
        flops += 2 * sum(entry[3] for entry in lifts) * frames * width * 3 * time.shape[1] * channels
    if fetched:
        scratch.append(pltpu.SemaphoreType.DMA((rows_in,)))
    if fetch:
        scratch += [pltpu.VMEM(weight.shape, jnp.bfloat16), pltpu.SemaphoreType.DMA((3,))]
        held += 2 * weight.size
    if edges:
        scratch.append(pltpu.SemaphoreType.DMA((len(edges),)))
    if staged:
        scratch += [pltpu.VMEM((rows_out, frames, width, channels), jnp.bfloat16), pltpu.SemaphoreType.DMA((1,))]
        held += 2 * frames * width * channels * rows_out
    return pl.pallas_call(
        functools.partial(stage_kernel, plan),
        out_shape=[jax.ShapeDtypeStruct(shape, jnp.bfloat16) for shape in out_shapes],
        in_specs=[pl.BlockSpec(memory_space=space) for space in spaces],
        out_specs=[pl.BlockSpec(memory_space=space) for space in out_spaces],
        scratch_shapes=scratch,
        input_output_aliases={} if into is None else {len(args) - 1: 0},
        compiler_params=pltpu.CompilerParams(vmem_limit_bytes=held + 12 * MIB),
        cost_estimate=pl.CostEstimate(flops=flops, bytes_accessed=1024, transcendentals=0),
        name=name,
    )(*args)


def to_next(value, axis):
    count = lax.axis_size(axis)
    return lax.ppermute(value, axis, [(i, i + 1) for i in range(count - 1)])


def to_previous(value, axis):
    count = lax.axis_size(axis)
    return lax.ppermute(value, axis, [(i + 1, i) for i in range(count - 1)])


def on_device(frames, space_weight, time_weight, out_weight):
    count, rows, width, channels = frames.shape
    depth = time_weight.shape[3]
    space = space_weight.reshape(3, 3 * channels, channels)
    time = time_weight.reshape(3, channels, 2 * depth)
    out_w = out_weight.reshape(3, 3 * depth, depth)
    wide = (count, width, channels)
    fine = (2 * count, width, depth)
    last = rows - 1

    def chunk(n):
        return (n, count, width, channels)

    def lifted(n):
        return (n, 2 * count, width, depth)

    here = pltpu.with_memory_space_constraint(frames, pltpu.HBM)
    space_here = pltpu.with_memory_space_constraint(space, pltpu.HBM)
    (ha,) = stage(
        "hidden_1_2", [here], space_here, [(0, 0, 4, 0)], [(0, 2, 0, 0, 0)], [chunk(2)], wide, fetched=True, fetch=True
    )
    pa = to_next(ha, "tm")
    (hb,) = stage(
        "hidden_3_6",
        [here],
        space,
        [(0, 2, 6, 0)],
        [(0, 4, 0, 0, 0)],
        [chunk(4)],
        wide,
        fetched=True,
        after=[ha],
    )
    pb = to_next(hb, "tm")
    hc, first_row, last_row = stage(
        "hidden_7_10",
        [here],
        space,
        [(0, 6, 6, 0)],
        [(0, 4, 0, 0, 0)],
        [chunk(4)],
        wide,
        fetched=True,
        after=[hb],
        edges=(0, last),
    )
    pc = to_next(hc, "tm")
    above = to_next(last_row, "rows")
    below = to_previous(first_row, "rows")
    hd, he, hf = stage(
        "hidden_rest",
        [here, above, below],
        space,
        [(1, 0, 1, 0), (0, 0, 2, 1), (0, 10, 6, 3), (2, 0, 1, 9)],
        [(0, 1, 0, 0, 1), (3, 2, 0, 1, 0), (5, 2, 2, 2, 0), (7, 1, 2, 0, 0)],
        [chunk(2), chunk(2), chunk(2)],
        wide,
        fetched=True,
        after=[hc, pa],
    )
    pd = to_next(hd, "tm")
    pe = to_next(he, "tm")
    pf = to_next(hf, "tm")

    whole = (2 * count, rows, width, depth)
    out, ua, ub = stage(
        "out_2_5",
        [ha, pa, hb, pb],
        out_w,
        [],
        [(0, 4, 0, 0, 2)],
        [whole, lifted(2), lifted(2)],
        fine,
        staged=True,
        lifts=[(0, 1, 0, 2, 0), (2, 3, 0, 4, 2)],
        time=time,
        keeps=[(1, 0, 2), (2, 4, 2)],
        after=[hd],
    )
    out, uc = stage(
        "out_6_9",
        [hc, pc, ub],
        out_w,
        [(2, 0, 2, 0)],
        [(0, 4, 0, 0, 6)],
        [whole, lifted(2)],
        fine,
        staged=True,
        lifts=[(0, 1, 0, 4, 2)],
        time=time,
        keeps=[(1, 4, 2)],
        into=out,
    )
    ud = upsample("up_edges", hd, pd, time, depth, uc)
    up_above = to_next(ud[:1], "rows")
    up_below = to_previous(ud[1:], "rows")
    out, ue = stage(
        "out_0_1_10_11",
        [he, pe, uc, ua, ud, up_above],
        out_w,
        [(2, 0, 2, 0), (5, 0, 1, 4), (4, 1, 1, 5), (3, 0, 2, 6)],
        [(0, 2, 0, 0, 10), (4, 2, 0, 0, 0)],
        [whole, lifted(2)],
        fine,
        staged=True,
        lifts=[(0, 1, 0, 2, 2)],
        time=time,
        keeps=[(1, 2, 2)],
        into=out,
    )
    (out,) = stage(
        "out_12_15",
        [hf, pf, ue, ud, up_below],
        out_w,
        [(2, 0, 2, 0), (3, 0, 1, 4), (4, 0, 1, 5)],
        [(0, 4, 0, 0, 12)],
        [whole],
        fine,
        staged=True,
        lifts=[(0, 1, 0, 2, 2)],
        time=time,
        into=out,
    )
    return out


def upsample_kernel(own_ref, prev_ref, w_ref, _, out_ref):
    rows, _, width, channels = own_ref.shape
    depth = out_ref.shape[3]
    size = rows * width
    window = [
        prev_ref[:, 0].reshape(size, channels),
        prev_ref[:, 1].reshape(size, channels),
        own_ref[:, 0].reshape(size, channels),
        own_ref[:, 1].reshape(size, channels),
    ]
    for frame in range(2):
        total = jnp.dot(window[frame], w_ref[0], preferred_element_type=jnp.float32)
        for tap in (1, 2):
            total += jnp.dot(window[frame + tap], w_ref[tap], preferred_element_type=jnp.float32)
        total = total.astype(jnp.bfloat16)
        for half in range(2):
            out_ref[:, 2 * frame + half] = total[:, half * depth : (half + 1) * depth].reshape(
                rows, width, depth
            )


def upsample(name, own, prev, weight, depth, after):
    rows, frames, width, channels = own.shape
    return pl.pallas_call(
        upsample_kernel,
        out_shape=jax.ShapeDtypeStruct((rows, 2 * frames, width, depth), jnp.bfloat16),
        in_specs=[pl.BlockSpec(memory_space=pltpu.VMEM)] * 3 + [pl.BlockSpec(memory_space=pltpu.HBM)],
        out_specs=pl.BlockSpec(memory_space=pltpu.VMEM),
        compiler_params=pltpu.CompilerParams(vmem_limit_bytes=12 * MIB),
        cost_estimate=pl.CostEstimate(
            flops=2 * rows * frames * width * 3 * channels * 2 * depth,
            bytes_accessed=2 * rows * frames * width * (2 * channels + 2 * depth) + 2 * weight.size,
            transcendentals=0,
        ),
        name=name,
    )(own, prev, weight, after)


def solution(mesh):
    return jax.shard_map(
        on_device,
        mesh=mesh,
        in_specs=(P("tm", "rows", None, None), P(), P(), P()),
        out_specs=P("tm", "rows", None, None),
        check_vma=False,
    )
```

profile of v0, /device:TPU:20, one launch (start us, length us, event | category | flops | bytes accessed | tf_op | source)
XLA Modules:
  0.0 105.8 jit_solution(9038761579832056085)
XLA Ops:
  0.0 0.0 copy-start
  0.0 5.4 %hidden_1_2.1.refs_2_.refs_0_ = bf16[2,2,128,512]{3,2,1,0:T(8,128)(2,1)S(1)} custom-call(bf16[2,16,128,512]{3,2,1,0:T(8,128)(2,1)} %refs_0_.7, bf16[3,1536,512]{2,1,0:T(8,128)(2,1)} %bitcast.2), custom_call_target="tpu_custom_call" | custom-call | flops 2415919104 | bytes 1024 | tf_op jit(solution)/shard_map/hidden_1_2/pallas_call | solution.py:232
  5.4 3.4 %collective-permute-start.2 = (bf16[2,2,128,512]{3,2,1,0:T(8,128)(2,1)S(1)}, bf16[2,2,128,512]{3,2,1,0:T(8,128)(2,1)}, u32[]{:S(2)}, u32[]{:S(2)}) collective-permute-start(bf16[2,2,128,512]{3,2,1,0:T(8,128)(2,1)S(1)} %hidden_1_2.1.refs_2_.refs_0_), channel_id=1, source_target_pairs={{0,8},{8,16},{16,24},{1,9},{9,17},{17,25},{2,10},{10,18},{18,26},{... | collective-permute-start | bytes 1572872 | tf_op jit(solution)/shard_map/ppermute | solution.py:247
  8.8 0.0 copy-done
  8.8 8.0 %hidden_3_6.1.refs_2_ = bf16[4,2,128,512]{3,2,1,0:T(8,128)(2,1)} custom-call(bf16[2,16,128,512]{3,2,1,0:T(8,128)(2,1)} %refs_0_.7, bf16[3,1536,512]{2,1,0:T(8,128)(2,1)S(1)} %bitcast.3, bf16[2,2,128,512]{3,2,1,0:T(8,128)(2,1)S(1)} %hidden_1_2.1.refs_2_.refs_0_), custom_call_target="tpu_custom_call" | custom-call | flops 4831838208 | bytes 1024 | tf_op jit(solution)/shard_map/hidden_3_6/pallas_call | solution.py:232
  16.8 1.9 %collective-permute-start.6 = (bf16[4,2,128,512]{3,2,1,0:T(8,128)(2,1)}, bf16[4,2,128,512]{3,2,1,0:T(8,128)(2,1)}, u32[]{:S(2)}, u32[]{:S(2)}) collective-permute-start(bf16[4,2,128,512]{3,2,1,0:T(8,128)(2,1)} %hidden_3_6.1.refs_2_), channel_id=1, source_target_pairs={{0,8},{8,16},{16,24},{1,9},{9,17},{17,25},{2,10},{10,18},{18,26},{... | collective-permute-start | bytes 3145736 | tf_op jit(solution)/shard_map/ppermute | solution.py:247
  18.7 8.2 %hidden_7_10.1 = (bf16[4,2,128,512]{3,2,1,0:T(8,128)(2,1)}, bf16[2,1,128,512]{3,2,1,0:T(8,128)(2,1)}, bf16[2,1,128,512]{3,2,1,0:T(8,128)(2,1)}) custom-call(bf16[2,16,128,512]{3,2,1,0:T(8,128)(2,1)} %refs_0_.7, bf16[3,1536,512]{2,1,0:T(8,128)(2,1)S(1)} %bitcast.4, bf16[4,2,128,512]{3,2,1,0:T(8,128)(2,1)} %hidden_3_6.1.refs_2_), custom_call_target="tpu_custom_call" | custom-call | flops 4831838208 | bytes 1024 | tf_op jit(solution)/shard_map/hidden_7_10/pallas_call | solution.py:232
  26.9 1.9 %collective-permute-start = (bf16[2,1,128,512]{3,2,1,0:T(8,128)(2,1)}, bf16[2,1,128,512]{3,2,1,0:T(8,128)(2,1)S(1)}, u32[]{:S(2)}, u32[]{:S(2)}) collective-permute-start(bf16[2,1,128,512]{3,2,1,0:T(8,128)(2,1)} %get-tuple-element.18), channel_id=1, source_target_pairs={{0,1},{1,2},{2,3},{3,4},{4,5},{5,6},{6,7},{8,9},{9,10},{10,11},{11... | collective-permute-start | bytes 786440 | tf_op jit(solution)/shard_map/ppermute | solution.py:247
  28.9 3.6 %collective-permute-start.1 = (bf16[2,1,128,512]{3,2,1,0:T(8,128)(2,1)}, bf16[2,1,128,512]{3,2,1,0:T(8,128)(2,1)}, u32[]{:S(2)}, u32[]{:S(2)}) collective-permute-start(bf16[2,1,128,512]{3,2,1,0:T(8,128)(2,1)} %get-tuple-element.19), channel_id=1, source_target_pairs={{1,0},{2,1},{3,2},{4,3},{5,4},{6,5},{7,6},{9,8},{10,9},{11,10},{12... | collective-permute-start | bytes 786440 | tf_op jit(solution)/shard_map/ppermute | solution.py:252
  32.5 2.1 %collective-permute-start.5 = (bf16[4,2,128,512]{3,2,1,0:T(8,128)(2,1)}, bf16[4,2,128,512]{3,2,1,0:T(8,128)(2,1)}, u32[]{:S(2)}, u32[]{:S(2)}) collective-permute-start(bf16[4,2,128,512]{3,2,1,0:T(8,128)(2,1)} %get-tuple-element.20.refs_4_.refs_0_), channel_id=1, source_target_pairs={{0,8},{8,16},{16,24},{1,9},{9,17},{17,25},{2,10},{10,18},{18,26},{... | collective-permute-start | bytes 3145736 | tf_op jit(solution)/shard_map/ppermute | solution.py:247
  34.6 0.0 copy-start.2
  34.6 2.9 %reshape.11.refs_5_.refs_4_.w_ref.refs_7_.refs_6_ = bf16[3,512,512]{2,1,0:T(8,128)(2,1)S(1)} reshape(bf16[3,512,2,256]{3,2,1,0:T(2,128)(2,1)} %param.6) | data formatting | bytes 3145728 | tf_op jit(solution)/shard_map/reshape | solution.py:259
  37.5 0.0 collective-permute-done.refs_1_
  37.5 0.0 collective-permute-done.1.refs_2_
  37.5 0.0 collective-permute-done.2.refs_5_.refs_1_
  37.5 0.0 copy-start.1
  37.6 2.3 %copy-done.1 = bf16[3,3,512,512]{3,2,1,0:T(8,128)(2,1)S(1)} copy-done((bf16[3,3,512,512]{3,2,1,0:T(8,128)(2,1)S(1)}, bf16[3,3,512,512]{3,2,1,0:T(8,128)(2,1)}, u32[]{:S(2)}) %copy-start.1) | copy-done | bytes 4718616
  39.9 10.8 %hidden_rest.1 = (bf16[2,2,128,512]{3,2,1,0:T(8,128)(2,1)S(1)}, bf16[2,2,128,512]{3,2,1,0:T(8,128)(2,1)S(1)}, bf16[2,2,128,512]{3,2,1,0:T(8,128)(2,1)S(1)}) custom-call(bf16[2,16,128,512]{3,2,1,0:T(8,128)(2,1)} %refs_0_.7, bf16[2,1,128,512]{3,2,1,0:T(8,128)(2,1)S(1)} %collective-permute-done.refs_1_, ...), custom_call_target="tpu_custom_call" | custom-call | flops 7247757312 | bytes 1024 | tf_op jit(solution)/shard_map/hidden_rest/pallas_call | solution.py:232
  50.7 1.9 %collective-permute-start.7 = (bf16[2,2,128,512]{3,2,1,0:T(8,128)(2,1)S(1)}, bf16[2,2,128,512]{3,2,1,0:T(8,128)(2,1)S(1)}, u32[]{:S(2)}, u32[]{:S(2)}) collective-permute-start(bf16[2,2,128,512]{3,2,1,0:T(8,128)(2,1)S(1)} %get-tuple-element.23.refs_6_.own_ref), channel_id=1, source_target_pairs={{0,8},{8,16},{16,24},{1,9},{9,17},{17,25},{2,10},{10,18},{18,26},{... | collective-permute-start | bytes 1572872 | tf_op jit(solution)/shard_map/ppermute | solution.py:247
  52.6 2.1 %collective-permute-start.4 = (bf16[2,2,128,512]{3,2,1,0:T(8,128)(2,1)S(1)}, bf16[2,2,128,512]{3,2,1,0:T(8,128)(2,1)S(1)}, u32[]{:S(2)}, u32[]{:S(2)}) collective-permute-start(bf16[2,2,128,512]{3,2,1,0:T(8,128)(2,1)S(1)} %get-tuple-element.22.refs_0_), channel_id=1, source_target_pairs={{0,8},{8,16},{16,24},{1,9},{9,17},{17,25},{2,10},{10,18},{18,26},{... | collective-permute-start | bytes 1572872 | tf_op jit(solution)/shard_map/ppermute | solution.py:247
  54.8 0.0 collective-permute-done.6.refs_3_
  54.8 0.0 copy-done.2
  54.8 9.0 %out_2_5.1 = (bf16[4,16,128,256]{3,2,1,0:T(8,128)(2,1)}, bf16[2,4,128,256]{3,2,1,0:T(8,128)(2,1)S(1)}, bf16[2,4,128,256]{3,2,1,0:T(8,128)(2,1)S(1)}) custom-call(bf16[2,2,128,512]{3,2,1,0:T(8,128)(2,1)S(1)} %hidden_1_2.1.refs_2_.refs_0_, bf16[2,2,128,512]{3,2,1,0:T(8,128)(2,1)} %collective-permute-done.2.refs_5_.refs_1_, ...), custom_call_target="tpu_custom_call" | custom-call | flops 4831838208 | bytes 1024 | tf_op jit(solution)/shard_map/out_2_5/pallas_call | solution.py:232
  63.9 4.6 %collective-permute-done.5.refs_1_ = bf16[4,2,128,512]{3,2,1,0:T(8,128)(2,1)} collective-permute-done((bf16[4,2,128,512]{3,2,1,0:T(8,128)(2,1)}, bf16[4,2,128,512]{3,2,1,0:T(8,128)(2,1)}, u32[]{:S(2)}, u32[]{:S(2)}) %collective-permute-start.5) | collective-permute-done | bytes 1048608 | tf_op jit(solution)/shard_map/ppermute | solution.py:247
  68.5 7.9 %out_6_9.1 = (bf16[4,16,128,256]{3,2,1,0:T(8,128)(2,1)}, bf16[2,4,128,256]{3,2,1,0:T(8,128)(2,1)S(1)}) custom-call(bf16[4,2,128,512]{3,2,1,0:T(8,128)(2,1)} %get-tuple-element.20.refs_4_.refs_0_, bf16[4,2,128,512]{3,2,1,0:T(8,128)(2,1)} %collective-permute-done.5.refs_1_, ...), custom_call_target="tpu_custom_call", output_to_operand_aliasing={{0}: (5, {})} | custom-call | flops 4026531840 | bytes 1024 | tf_op jit(solution)/shard_map/out_6_9/pallas_call | solution.py:232
  76.4 3.2 %collective-permute-done.7.prev_ref = bf16[2,2,128,512]{3,2,1,0:T(8,128)(2,1)S(1)} collective-permute-done((bf16[2,2,128,512]{3,2,1,0:T(8,128)(2,1)S(1)}, bf16[2,2,128,512]{3,2,1,0:T(8,128)(2,1)S(1)}, u32[]{:S(2)}, u32[]{:S(2)}) %collective-permute-start.7) | collective-permute-done | bytes 524320 | tf_op jit(solution)/shard_map/ppermute | solution.py:247
  79.6 1.0 up_edges.1.refs_4_.refs_3_
  80.6 1.9 %collective-permute-start.8 = (bf16[1,4,128,256]{3,2,1,0:T(8,128)(2,1)S(1)}, bf16[1,4,128,256]{3,2,1,0:T(8,128)(2,1)S(1)}, u32[]{:S(2)}, u32[]{:S(2)}) collective-permute-start(bf16[1,4,128,256]{3,2,1,0:T(8,128)(2,1)S(1)} %get-tuple-element.32), channel_id=1, source_target_pairs={{0,1},{1,2},{2,3},{3,4},{4,5},{5,6},{6,7},{8,9},{9,10},{10,11},{11... | collective-permute-start | bytes 786440 | tf_op jit(solution)/shard_map/ppermute | solution.py:247
  82.6 1.9 %collective-permute-start.3 = (bf16[2,2,128,512]{3,2,1,0:T(8,128)(2,1)S(1)}, bf16[2,2,128,512]{3,2,1,0:T(8,128)(2,1)S(1)}, u32[]{:S(2)}, u32[]{:S(2)}) collective-permute-start(bf16[2,2,128,512]{3,2,1,0:T(8,128)(2,1)S(1)} %get-tuple-element.21.refs_0_), channel_id=1, source_target_pairs={{0,8},{8,16},{16,24},{1,9},{9,17},{17,25},{2,10},{10,18},{18,26},{... | collective-permute-start | bytes 1572872 | tf_op jit(solution)/shard_map/ppermute | solution.py:247
  84.5 3.9 %collective-permute-start.9 = (bf16[1,4,128,256]{3,2,1,0:T(8,128)(2,1)S(1)}, bf16[1,4,128,256]{3,2,1,0:T(8,128)(2,1)S(1)}, u32[]{:S(2)}, u32[]{:S(2)}) collective-permute-start(bf16[1,4,128,256]{3,2,1,0:T(8,128)(2,1)S(1)} %get-tuple-element.31), channel_id=1, source_target_pairs={{1,0},{2,1},{3,2},{4,3},{5,4},{6,5},{7,6},{9,8},{10,9},{11,10},{12... | collective-permute-start | bytes 786440 | tf_op jit(solution)/shard_map/ppermute | solution.py:252
  88.4 1.0 collective-permute-done.4.refs_1_
  89.4 0.0 collective-permute-done.8.refs_5_
  89.4 8.5 %out_0_1_10_11.1 = (bf16[4,16,128,256]{3,2,1,0:T(8,128)(2,1)}, bf16[2,4,128,256]{3,2,1,0:T(8,128)(2,1)S(1)}) custom-call(bf16[2,2,128,512]{3,2,1,0:T(8,128)(2,1)S(1)} %get-tuple-element.22.refs_0_, bf16[2,2,128,512]{3,2,1,0:T(8,128)(2,1)S(1)} %collective-permute-done.4.refs_1_, ...), custom_call_target="tpu_custom_call", output_to_operand_aliasing={{0}: (8, {})} | custom-call | flops 3221225472 | bytes 1024 | tf_op jit(solution)/shard_map/out_0_1_10_11/pallas_call | solution.py:232
  97.9 2.4 %collective-permute-done.3.refs_1_ = bf16[2,2,128,512]{3,2,1,0:T(8,128)(2,1)S(1)} collective-permute-done((bf16[2,2,128,512]{3,2,1,0:T(8,128)(2,1)S(1)}, bf16[2,2,128,512]{3,2,1,0:T(8,128)(2,1)S(1)}, u32[]{:S(2)}, u32[]{:S(2)}) %collective-permute-start.3) | collective-permute-done | bytes 524320 | tf_op jit(solution)/shard_map/ppermute | solution.py:247
  100.3 0.0 collective-permute-done.9.refs_4_
  100.3 5.3 %out_12_15.1 = bf16[4,16,128,256]{3,2,1,0:T(8,128)(2,1)} custom-call(bf16[2,2,128,512]{3,2,1,0:T(8,128)(2,1)S(1)} %get-tuple-element.21.refs_0_, bf16[2,2,128,512]{3,2,1,0:T(8,128)(2,1)S(1)} %collective-permute-done.3.refs_1_, bf16[2,4,128,256]{3,2,1,0:T(8,128)(2,1)S(1)} %get-tuple-element.29.refs_2_, ...), custom_call_target="tpu_custom_call", output_to_operand_aliasing={{}: (7, {})} | custom-call | flops 3221225472 | bytes 1024 | tf_op jit(solution)/shard_map/out_12_15/pallas_call | solution.py:232
  (1 shorter events, 0.0 us)
Async XLA Ops:
  0.0 8.8 %copy-start = (bf16[3,3,512,512]{3,2,1,0:T(8,128)(2,1)S(1)}, bf16[3,3,512,512]{3,2,1,0:T(8,128)(2,1)}, u32[]{:S(2)}) copy-start(bf16[3,3,512,512]{3,2,1,0:T(8,128)(2,1)} %param.5) | copy-start | bytes 14155780
  5.4 32.2 %collective-permute-start.2 = (bf16[2,2,128,512]{3,2,1,0:T(8,128)(2,1)S(1)}, bf16[2,2,128,512]{3,2,1,0:T(8,128)(2,1)}, u32[]{:S(2)}, u32[]{:S(2)}) collective-permute-start(bf16[2,2,128,512]{3,2,1,0:T(8,128)(2,1)S(1)} %hidden_1_2.1.refs_2_.refs_0_), channel_id=1, source_target_pairs={{0,8},{8,16},{16,24},{1,9},{9,17},{17,25},{2,10},{10,18},{18,26},{... | collective-permute-start | bytes 1572872 | tf_op jit(solution)/shard_map/ppermute | solution.py:247
  16.8 38.0 %collective-permute-start.6 = (bf16[4,2,128,512]{3,2,1,0:T(8,128)(2,1)}, bf16[4,2,128,512]{3,2,1,0:T(8,128)(2,1)}, u32[]{:S(2)}, u32[]{:S(2)}) collective-permute-start(bf16[4,2,128,512]{3,2,1,0:T(8,128)(2,1)} %hidden_3_6.1.refs_2_), channel_id=1, source_target_pairs={{0,8},{8,16},{16,24},{1,9},{9,17},{17,25},{2,10},{10,18},{18,26},{... | collective-permute-start | bytes 3145736 | tf_op jit(solution)/shard_map/ppermute | solution.py:247
  26.9 10.6 %collective-permute-start = (bf16[2,1,128,512]{3,2,1,0:T(8,128)(2,1)}, bf16[2,1,128,512]{3,2,1,0:T(8,128)(2,1)S(1)}, u32[]{:S(2)}, u32[]{:S(2)}) collective-permute-start(bf16[2,1,128,512]{3,2,1,0:T(8,128)(2,1)} %get-tuple-element.18), channel_id=1, source_target_pairs={{0,1},{1,2},{2,3},{3,4},{4,5},{5,6},{6,7},{8,9},{9,10},{10,11},{11... | collective-permute-start | bytes 786440 | tf_op jit(solution)/shard_map/ppermute | solution.py:247
  28.9 8.7 %collective-permute-start.1 = (bf16[2,1,128,512]{3,2,1,0:T(8,128)(2,1)}, bf16[2,1,128,512]{3,2,1,0:T(8,128)(2,1)}, u32[]{:S(2)}, u32[]{:S(2)}) collective-permute-start(bf16[2,1,128,512]{3,2,1,0:T(8,128)(2,1)} %get-tuple-element.19), channel_id=1, source_target_pairs={{1,0},{2,1},{3,2},{4,3},{5,4},{6,5},{7,6},{9,8},{10,9},{11,10},{12... | collective-permute-start | bytes 786440 | tf_op jit(solution)/shard_map/ppermute | solution.py:252
  32.5 36.0 %collective-permute-start.5 = (bf16[4,2,128,512]{3,2,1,0:T(8,128)(2,1)}, bf16[4,2,128,512]{3,2,1,0:T(8,128)(2,1)}, u32[]{:S(2)}, u32[]{:S(2)}) collective-permute-start(bf16[4,2,128,512]{3,2,1,0:T(8,128)(2,1)} %get-tuple-element.20.refs_4_.refs_0_), channel_id=1, source_target_pairs={{0,8},{8,16},{16,24},{1,9},{9,17},{17,25},{2,10},{10,18},{18,26},{... | collective-permute-start | bytes 3145736 | tf_op jit(solution)/shard_map/ppermute | solution.py:247
  34.6 20.2 %copy-start.2 = (bf16[3,3,256,256]{3,2,1,0:T(8,128)(2,1)S(1)}, bf16[3,3,256,256]{3,2,1,0:T(8,128)(2,1)}, u32[]{:S(2)}) copy-start(bf16[3,3,256,256]{3,2,1,0:T(8,128)(2,1)} %param.7) | copy-start | bytes 3538948
  37.5 2.3 %copy-start.1 = (bf16[3,3,512,512]{3,2,1,0:T(8,128)(2,1)S(1)}, bf16[3,3,512,512]{3,2,1,0:T(8,128)(2,1)}, u32[]{:S(2)}) copy-start(bf16[3,3,512,512]{3,2,1,0:T(8,128)(2,1)} %param.5) | copy-start | bytes 14155780
  50.7 28.9 %collective-permute-start.7 = (bf16[2,2,128,512]{3,2,1,0:T(8,128)(2,1)S(1)}, bf16[2,2,128,512]{3,2,1,0:T(8,128)(2,1)S(1)}, u32[]{:S(2)}, u32[]{:S(2)}) collective-permute-start(bf16[2,2,128,512]{3,2,1,0:T(8,128)(2,1)S(1)} %get-tuple-element.23.refs_6_.own_ref), channel_id=1, source_target_pairs={{0,8},{8,16},{16,24},{1,9},{9,17},{17,25},{2,10},{10,18},{18,26},{... | collective-permute-start | bytes 1572872 | tf_op jit(solution)/shard_map/ppermute | solution.py:247
  52.6 36.7 %collective-permute-start.4 = (bf16[2,2,128,512]{3,2,1,0:T(8,128)(2,1)S(1)}, bf16[2,2,128,512]{3,2,1,0:T(8,128)(2,1)S(1)}, u32[]{:S(2)}, u32[]{:S(2)}) collective-permute-start(bf16[2,2,128,512]{3,2,1,0:T(8,128)(2,1)S(1)} %get-tuple-element.22.refs_0_), channel_id=1, source_target_pairs={{0,8},{8,16},{16,24},{1,9},{9,17},{17,25},{2,10},{10,18},{18,26},{... | collective-permute-start | bytes 1572872 | tf_op jit(solution)/shard_map/ppermute | solution.py:247
  80.6 8.8 %collective-permute-start.8 = (bf16[1,4,128,256]{3,2,1,0:T(8,128)(2,1)S(1)}, bf16[1,4,128,256]{3,2,1,0:T(8,128)(2,1)S(1)}, u32[]{:S(2)}, u32[]{:S(2)}) collective-permute-start(bf16[1,4,128,256]{3,2,1,0:T(8,128)(2,1)S(1)} %get-tuple-element.32), channel_id=1, source_target_pairs={{0,1},{1,2},{2,3},{3,4},{4,5},{5,6},{6,7},{8,9},{9,10},{10,11},{11... | collective-permute-start | bytes 786440 | tf_op jit(solution)/shard_map/ppermute | solution.py:247
  82.6 17.7 %collective-permute-start.3 = (bf16[2,2,128,512]{3,2,1,0:T(8,128)(2,1)S(1)}, bf16[2,2,128,512]{3,2,1,0:T(8,128)(2,1)S(1)}, u32[]{:S(2)}, u32[]{:S(2)}) collective-permute-start(bf16[2,2,128,512]{3,2,1,0:T(8,128)(2,1)S(1)} %get-tuple-element.21.refs_0_), channel_id=1, source_target_pairs={{0,8},{8,16},{16,24},{1,9},{9,17},{17,25},{2,10},{10,18},{18,26},{... | collective-permute-start | bytes 1572872 | tf_op jit(solution)/shard_map/ppermute | solution.py:247
  84.5 15.8 %collective-permute-start.9 = (bf16[1,4,128,256]{3,2,1,0:T(8,128)(2,1)S(1)}, bf16[1,4,128,256]{3,2,1,0:T(8,128)(2,1)S(1)}, u32[]{:S(2)}, u32[]{:S(2)}) collective-permute-start(bf16[1,4,128,256]{3,2,1,0:T(8,128)(2,1)S(1)} %get-tuple-element.31), channel_id=1, source_target_pairs={{1,0},{2,1},{3,2},{4,3},{5,4},{6,5},{7,6},{9,8},{10,9},{11,10},{12... | collective-permute-start | bytes 786440 | tf_op jit(solution)/shard_map/ppermute | solution.py:252
where the time goes:
time: 107 us; the launch traced here: 106 us
  Pallas kernels  64.1 us (60%)
  starting transfers between devices  24.8 us (23%)
  waiting for transfers between devices  11.3 us (11%)
  local copies, waits for them, and re-layouts  5.24 us (5%)
    pallas_call x8, Pallas kernels, stage(): pl.pallas_call(functools.partial(stage_kernel, plan), out_shape=[jax.Shap...  63.1 us
    ppermute x8, starting transfers between devices, to_next(): return lax.ppermute(value, axis, [(i, i + 1) for i in range(count - 1)])  17.2 us
    ppermute x8, waiting for transfers between devices, to_next(): return lax.ppermute(value, axis, [(i, i + 1) for i in range(count - 1)])  11.3 us
    ppermute x2, starting transfers between devices, to_previous(): return lax.ppermute(value, axis, [(i + 1, i) for i in range(count - 1)])  7.55 us
    reshape x1, local copies, waits for them, and re-layouts, on_device(): time = time_weight.reshape(3, channels, 2 * depth)  2.87 us
    unnamed x6, local copies, waits for them, and re-layouts  2.34 us
  transfers between devices with their start and end apart: 10, of which 4 were waited for; matrix products, arithmetic and copies ran while one was open for 3% of the time, Pallas kernels for 50%

commit v1 on v0

--- a/solution.py
+++ b/solution.py
@@ -30,14 +30,27 @@
             )
 
 
-def convolve(x_ref, act_ref, w_ref, out_ref, source, target, group, between):
+def convolve(x_ref, act_ref, w_ref, out_ref, source, target, group, between, parts=None):
     _, frames, width, channels = x_ref.shape
     size = group * frames * width
-    total = x_ref[pl.ds(source + 1, group)].reshape(size, channels).astype(jnp.float32)
+    total = None
     for tap in range(3):
         between(tap)
-        lhs = act_ref[pl.ds(source + tap, group)].reshape(size, 3 * channels)
-        total += jnp.dot(lhs, w_ref[tap], preferred_element_type=jnp.float32)
+        if parts is None:
+            lhs = act_ref[pl.ds(source + tap, group)].reshape(size, 3 * channels)
+            part = jnp.dot(lhs, w_ref[tap], preferred_element_type=jnp.float32)
+            total = part if total is None else total + part
+            continue
+        for column in range(3):
+            parts[3 * tap + column].wait()
+            if tap == 0 and column == 2:
+                for copy in parts[6:]:
+                    copy.start()
+            span = slice(column * channels, (column + 1) * channels)
+            lhs = act_ref[pl.ds(source + tap, group), :, :, span].reshape(size, channels)
+            part = jnp.dot(lhs, w_ref[tap, span], preferred_element_type=jnp.float32)
+            total = part if total is None else total + part
+    total += x_ref[pl.ds(source + 1, group)].reshape(size, channels).astype(jnp.float32)
     out_ref[pl.ds(target, group)] = total.astype(jnp.bfloat16).reshape(group, frames, width, channels)
 
 
@@ -62,6 +75,14 @@
             )
 
 
+def lift_own(own_ref, time_ref, out_ref):
+    first, second = own_ref[0, 0], own_ref[0, 1]
+    out_ref[0] = jnp.dot(first, time_ref[2], preferred_element_type=jnp.float32)
+    out_ref[1] = jnp.dot(first, time_ref[1], preferred_element_type=jnp.float32) + jnp.dot(
+        second, time_ref[2], preferred_element_type=jnp.float32
+    )
+
+
 def stage_kernel(plan, *refs):
     refs = list(refs)
     sources = [refs.pop(0) for _ in range(plan["sources"])]
@@ -86,7 +107,16 @@
     if plan["fetch"]:
         w_hbm = w_ref
         w_ref, w_sem = [refs.pop(0) for _ in range(2)]
-        weights = [pltpu.make_async_copy(w_hbm.at[tap], w_ref.at[tap], w_sem.at[tap]) for tap in range(3)]
+        depth = x_ref.shape[3]
+        weights = [
+            pltpu.make_async_copy(
+                w_hbm.at[tap, pl.ds(column * depth, depth)],
+                w_ref.at[tap, pl.ds(column * depth, depth)],
+                w_sem.at[3 * tap + column],
+            )
+            for tap in range(3)
+            for column in range(3)
+        ]
     edges = []
     if plan["edges"]:
         edge_sem = refs.pop(0)
@@ -96,7 +126,7 @@
             )
             for number, row in enumerate(plan["edges"])
         ]
-    for copy in weights + edges:
+    for copy in weights[:3] + edges:
         copy.start()
     if plan["staged"]:
         stage_ref, out_sem = [refs.pop(0) for _ in range(2)]
@@ -122,22 +152,39 @@
             pltpu.make_async_copy(x_ref.at[row], x_ref.at[row], in_sem.at[row]).wait()
         activate(x_ref, act_ref, row, frame)
 
+    def partial_sums():
+        size = frames * x_ref.shape[2]
+        for row in plan["prepared"]:
+            for frame in range(frames):
+                prepare(row, frame)
+        for out, index, residual, taps in plan["partials"]:
+            total = None
+            for tap, row in taps:
+                lhs = act_ref[row].reshape(size, 3 * x_ref.shape[3])
+                part = jnp.dot(lhs, w_ref[tap], preferred_element_type=jnp.float32)
+                total = part if total is None else total + part
+            if residual is not None:
+                total += x_ref[residual].reshape(size, x_ref.shape[3]).astype(jnp.float32)
+            outs[out][index] = total.reshape(x_ref.shape[1:])
+        if plan["own_part"] is not None:
+            source, out = plan["own_part"]
+            lift_own(sources[source], time_ref, outs[out])
+
     target = 0
     for number, (source, count, active, out, start) in enumerate(plan["runs"]):
         group = min(count, 2)
         steps = count // group
 
-        def first(row, carry, source=source):
-            for frame in range(frames):
-                prepare(source + row, frame)
-            return carry
-
-        lax.fori_loop(active, group + 2, first, 0)
-
-        def body(step, carry, last, source=source, target=target, group=group, out=out, start=start):
+        def body(step, carry, first, last, source=source, target=target, group=group, out=out, start=start):
             def between(tap):
-                if weights and number == 0 and last:
-                    weights[tap].wait()
+                if first:
+                    for row in range(0, group) if tap == 0 else range(group + tap - 1, group + tap):
+                        if row >= active:
+                            for frame in range(frames):
+                                prepare(source + row, frame)
+                if first and tap == 0 and number == 0:
+                    for copy in weights[3:6]:
+                        copy.start()
                 if last:
                     return
                 for at, (row, frame) in enumerate((r, f) for r in range(group) for f in range(frames)):
@@ -146,7 +193,8 @@
 
             row = target + step * group if plan["staged"] else start + step * group
             to_ref = stage_ref if plan["staged"] else outs[out]
-            convolve(x_ref, act_ref, w_ref, to_ref, source + step * group, row, group, between)
+            parts = weights if weights and number == 0 and first else None
+            convolve(x_ref, act_ref, w_ref, to_ref, source + step * group, row, group, between, parts)
             if plan["staged"]:
                 for frame in range(frames):
                     pltpu.make_async_copy(
@@ -156,11 +204,14 @@
                     ).start()
             return carry
 
+        body(0, 0, first=True, last=steps == 1)
+        if steps > 2:
+            lax.fori_loop(1, steps - 1, functools.partial(body, first=False, last=False), 0)
         if steps > 1:
-            lax.fori_loop(0, steps - 1, functools.partial(body, last=False), 0)
-        body(steps - 1, 0, last=True)
+            body(steps - 1, 0, first=False, last=True)
         target += count
 
+    partial_sums()
     if plan["staged"]:
         pltpu.make_async_copy(stage_ref, stage_ref, out_sem.at[0]).wait()
     for copy in edges:
@@ -184,6 +235,9 @@
     after=(),
     edges=(),
     fetch=False,
+    prepared=(),
+    partials=(),
+    own_part=None,
 ):
     frames, width, channels = dims
     rows_in = max(target + count for *_, count, target in list(loads) + list(lifts))
@@ -210,7 +264,11 @@
         runs=runs,
         edges=edges,
         fetch=fetch,
-    )
+        prepared=prepared,
+        partials=partials,
+        own_part=own_part,
+    )
+    in_float = {entry[0] for entry in partials} | ({own_part[1]} if own_part else set())
     scratch = [
         pltpu.VMEM((rows_in, frames, width, channels), jnp.bfloat16),
         pltpu.VMEM((rows_in, frames, width, 3 * channels), jnp.bfloat16),
@@ -222,7 +280,7 @@
     if fetched:
         scratch.append(pltpu.SemaphoreType.DMA((rows_in,)))
     if fetch:
-        scratch += [pltpu.VMEM(weight.shape, jnp.bfloat16), pltpu.SemaphoreType.DMA((3,))]
+        scratch += [pltpu.VMEM(weight.shape, jnp.bfloat16), pltpu.SemaphoreType.DMA((9,))]
         held += 2 * weight.size
     if edges:
         scratch.append(pltpu.SemaphoreType.DMA((len(edges),)))
@@ -231,7 +289,10 @@
         held += 2 * frames * width * channels * rows_out
     return pl.pallas_call(
         functools.partial(stage_kernel, plan),
-        out_shape=[jax.ShapeDtypeStruct(shape, jnp.bfloat16) for shape in out_shapes],
+        out_shape=[
+            jax.ShapeDtypeStruct(shape, jnp.float32 if number in in_float else jnp.bfloat16)
+            for number, shape in enumerate(out_shapes)
+        ],
         in_specs=[pl.BlockSpec(memory_space=space) for space in spaces],
         out_specs=[pl.BlockSpec(memory_space=space) for space in out_spaces],
         scratch_shapes=scratch,
@@ -240,6 +301,57 @@
         cost_estimate=pl.CostEstimate(flops=flops, bytes_accessed=1024, transcendentals=0),
         name=name,
     )(*args)
+
+
+def finish_kernel(pair_ref, own_ref, part_ref, time_ref, w_ref, _, out_ref, x_ref, act_ref, stage_ref, sem, *, start):
+    frames, width, channels = x_ref.shape[1:]
+    before, latest = pair_ref[0, 0], pair_ref[0, 1]
+    for pair in range(2):
+        total = own_ref[pair]
+        if pair == 0:
+            total += jnp.dot(before, time_ref[0], preferred_element_type=jnp.float32)
+            total += jnp.dot(latest, time_ref[1], preferred_element_type=jnp.float32)
+        else:
+            total += jnp.dot(latest, time_ref[0], preferred_element_type=jnp.float32)
+        total = total.astype(jnp.bfloat16)
+        for half in range(2):
+            x_ref[0, 2 * pair + half] = total[:, half * channels : (half + 1) * channels]
+            activate(x_ref, act_ref, 0, 2 * pair + half)
+    copies = []
+    for row in range(3):
+        total = jnp.dot(
+            act_ref[0].reshape(frames * width, 3 * channels), w_ref[2 - row], preferred_element_type=jnp.float32
+        ).reshape(frames, width, channels)
+        total += part_ref[row]
+        if row == 1:
+            total += x_ref[0].astype(jnp.float32)
+        stage_ref[row] = total.astype(jnp.bfloat16)
+        copies.append(pltpu.make_async_copy(stage_ref.at[row], out_ref.at[:, start + row], sem.at[row]))
+        copies[-1].start()
+    for copy in copies:
+        copy.wait()
+
+
+def finish(name, pair, own, part, time, weight, into, start):
+    rows, frames, width, channels = part.shape
+    return pl.pallas_call(
+        functools.partial(finish_kernel, start=start),
+        out_shape=jax.ShapeDtypeStruct(into.shape, into.dtype),
+        in_specs=[pl.BlockSpec(memory_space=pltpu.VMEM)] * 5 + [pl.BlockSpec(memory_space=pl.ANY)],
+        out_specs=pl.BlockSpec(memory_space=pltpu.HBM),
+        scratch_shapes=[
+            pltpu.VMEM((1, frames, width, channels), jnp.bfloat16),
+            pltpu.VMEM((1, frames, width, 3 * channels), jnp.bfloat16),
+            pltpu.VMEM((rows, frames, width, channels), jnp.bfloat16),
+            pltpu.SemaphoreType.DMA((rows,)),
+        ],
+        input_output_aliases={5: 0},
+        compiler_params=pltpu.CompilerParams(vmem_limit_bytes=12 * MIB),
+        cost_estimate=pl.CostEstimate(
+            flops=2 * frames * width * channels * (9 * channels + 2 * time.shape[1]), bytes_accessed=1024, transcendentals=0
+        ),
+        name=name,
+    )(pair, own, part, time, weight, into)
 
 
 def to_next(value, axis):
@@ -306,8 +418,8 @@
         [here, above, below],
         space,
         [(1, 0, 1, 0), (0, 0, 2, 1), (0, 10, 6, 3), (2, 0, 1, 9)],
-        [(0, 1, 0, 0, 1), (3, 2, 0, 1, 0), (5, 2, 2, 2, 0), (7, 1, 2, 0, 0)],
-        [chunk(2), chunk(2), chunk(2)],
+        [(0, 1, 0, 0, 1), (3, 2, 0, 1, 0), (5, 1, 2, 2, 0), (6, 1, 2, 1, 2), (7, 1, 2, 0, 0)],
+        [chunk(2), chunk(3), chunk(1)],
         wide,
         fetched=True,
         after=[hc, pa],
@@ -348,34 +460,37 @@
     ud = upsample("up_edges", hd, pd, time, depth, uc)
     up_above = to_next(ud[:1], "rows")
     up_below = to_previous(ud[1:], "rows")
-    out, ue = stage(
-        "out_0_1_10_11",
-        [he, pe, uc, ua, ud, up_above],
+    (out,) = stage(
+        "out_0_1",
+        [ua, ud, up_above],
         out_w,
-        [(2, 0, 2, 0), (5, 0, 1, 4), (4, 1, 1, 5), (3, 0, 2, 6)],
-        [(0, 2, 0, 0, 10), (4, 2, 0, 0, 0)],
-        [whole, lifted(2)],
-        fine,
-        staged=True,
-        lifts=[(0, 1, 0, 2, 2)],
-        time=time,
-        keeps=[(1, 2, 2)],
-        into=out,
-    )
-    (out,) = stage(
-        "out_12_15",
-        [hf, pf, ue, ud, up_below],
-        out_w,
-        [(2, 0, 2, 0), (3, 0, 1, 4), (4, 0, 1, 5)],
-        [(0, 4, 0, 0, 12)],
+        [(2, 0, 1, 0), (1, 1, 1, 1), (0, 0, 2, 2)],
+        [(0, 2, 0, 0, 0)],
         [whole],
         fine,
         staged=True,
-        lifts=[(0, 1, 0, 2, 2)],
+        into=out,
+    )
+    out, part, own_part = stage(
+        "out_10_15",
+        [he, pe, uc, ud, up_below, hf],
+        out_w,
+        [(2, 0, 2, 0), (3, 0, 1, 5), (4, 0, 1, 6)],
+        [(0, 2, 0, 0, 10), (4, 1, 0, 0, 15)],
+        [whole, (3,) + lifted(1)[1:], (2, width, 2 * depth)],
+        fine,
+        staged=True,
+        lifts=[(0, 1, 0, 2, 2), (0, 1, 2, 1, 4)],
         time=time,
         into=out,
-    )
-    return out
+        partials=[
+            (1, 0, 3, ((0, 2), (1, 3))),
+            (1, 1, None, ((0, 3), (2, 4))),
+            (1, 2, 4, ((1, 4), (2, 5))),
+        ],
+        own_part=(5, 2),
+    )
+    return finish("out_12_14", pf, own_part, part, time, out_w, out, 12)
 
 
 def upsample_kernel(own_ref, prev_ref, w_ref, _, out_ref):

time: 107 us -> 103 us (0.963)
  Pallas kernels: 64.1 us -> 56.3 us
  waiting for transfers between devices: 11.3 us -> 15.2 us
    pallas_call x8, Pallas kernels: 63.1 us -> 53.4 us  [stage(): pl.pallas_call(functools.partial(stage_kernel, plan), out_shape=[jax.Shap...]
    ppermute x8, waiting for transfers between devices: 11.3 us -> 15.2 us  [to_next(): return lax.ppermute(value, axis, [(i, i + 1) for i in range(count - 1)])]
    pallas_call x0 -> x1, Pallas kernels: none -> 1.94 us  [finish(): pl.pallas_call(functools.partial(finish_kernel, start=start), out_shape=j...]
  transfers between devices with their start and end apart: 10 -> 10, of which waited for: 4 -> 3; matrix products, arithmetic and copies ran while one was open for 3% -> 3% of each run, Pallas kernels for 50% -> 48%
where the time goes in v1:
time: 103 us
  Pallas kernels  56.3 us (55%)
  starting transfers between devices  25.5 us (25%)
  waiting for transfers between devices  15.2 us (15%)
  local copies, waits for them, and re-layouts  5.24 us (5%)
    pallas_call x8, Pallas kernels, stage(): pl.pallas_call(functools.partial(stage_kernel, plan), out_shape=[jax.Shap...  53.4 us
    ppermute x8, starting transfers between devices, to_next(): return lax.ppermute(value, axis, [(i, i + 1) for i in range(count - 1)])  18.2 us
    ppermute x8, waiting for transfers between devices, to_next(): return lax.ppermute(value, axis, [(i, i + 1) for i in range(count - 1)])  15.2 us
    ppermute x2, starting transfers between devices, to_previous(): return lax.ppermute(value, axis, [(i + 1, i) for i in range(count - 1)])  7.29 us
    reshape x1, local copies, waits for them, and re-layouts, on_device(): time = time_weight.reshape(3, channels, 2 * depth)  2.77 us
    unnamed x6, local copies, waits for them, and re-layouts  2.43 us
  transfers between devices with their start and end apart: 10, of which 3 were waited for; matrix products, arithmetic and copies ran while one was open for 3% of the time, Pallas kernels for 48%

profile of v1, /device:TPU:20, one launch (start us, length us, event | category | flops | bytes accessed | tf_op | source)
XLA Modules:
  0.0 102.8 jit_solution(12034962035603631444)
XLA Ops:
  0.0 0.0 copy-start.1
  0.0 5.2 %hidden_1_2.1.refs_2_.refs_0_ = bf16[2,2,128,512]{3,2,1,0:T(8,128)(2,1)S(1)} custom-call(bf16[2,16,128,512]{3,2,1,0:T(8,128)(2,1)} %refs_0_.7, bf16[3,1536,512]{2,1,0:T(8,128)(2,1)} %bitcast.7), custom_call_target="tpu_custom_call" | custom-call | flops 2415919104 | bytes 1024 | tf_op jit(solution)/shard_map/hidden_1_2/pallas_call | solution.py:290
  5.2 3.4 %collective-permute-start.2 = (bf16[2,2,128,512]{3,2,1,0:T(8,128)(2,1)S(1)}, bf16[2,2,128,512]{3,2,1,0:T(8,128)(2,1)}, u32[]{:S(2)}, u32[]{:S(2)}) collective-permute-start(bf16[2,2,128,512]{3,2,1,0:T(8,128)(2,1)S(1)} %hidden_1_2.1.refs_2_.refs_0_), channel_id=1, source_target_pairs={{0,8},{8,16},{16,24},{1,9},{9,17},{17,25},{2,10},{10,18},{18,26},{... | collective-permute-start | bytes 1572872 | tf_op jit(solution)/shard_map/ppermute | solution.py:359
  8.6 0.0 copy-done.1
  8.6 7.1 %hidden_3_6.1.refs_2_ = bf16[4,2,128,512]{3,2,1,0:T(8,128)(2,1)S(1)} custom-call(bf16[2,16,128,512]{3,2,1,0:T(8,128)(2,1)} %refs_0_.7, bf16[3,1536,512]{2,1,0:T(8,128)(2,1)S(1)} %bitcast.8, bf16[2,2,128,512]{3,2,1,0:T(8,128)(2,1)S(1)} %hidden_1_2.1.refs_2_.refs_0_), custom_call_target="tpu_custom_call" | custom-call | flops 4831838208 | bytes 1024 | tf_op jit(solution)/shard_map/hidden_3_6/pallas_call | solution.py:290
  15.7 1.9 %collective-permute-start.6 = (bf16[4,2,128,512]{3,2,1,0:T(8,128)(2,1)S(1)}, bf16[4,2,128,512]{3,2,1,0:T(8,128)(2,1)}, u32[]{:S(2)}, u32[]{:S(2)}) collective-permute-start(bf16[4,2,128,512]{3,2,1,0:T(8,128)(2,1)S(1)} %hidden_3_6.1.refs_2_), channel_id=1, source_target_pairs={{0,8},{8,16},{16,24},{1,9},{9,17},{17,25},{2,10},{10,18},{18,26},{... | collective-permute-start | bytes 3145736 | tf_op jit(solution)/shard_map/ppermute | solution.py:359
  17.6 8.2 %hidden_7_10.1 = (bf16[4,2,128,512]{3,2,1,0:T(8,128)(2,1)}, bf16[2,1,128,512]{3,2,1,0:T(8,128)(2,1)}, bf16[2,1,128,512]{3,2,1,0:T(8,128)(2,1)}) custom-call(bf16[2,16,128,512]{3,2,1,0:T(8,128)(2,1)} %refs_0_.7, bf16[3,1536,512]{2,1,0:T(8,128)(2,1)S(1)} %bitcast.9, bf16[4,2,128,512]{3,2,1,0:T(8,128)(2,1)S(1)} %hidden_3_6.1.refs_2_), custom_call_target="tpu_custom_call" | custom-call | flops 4831838208 | bytes 1024 | tf_op jit(solution)/shard_map/hidden_7_10/pallas_call | solution.py:290
  25.8 1.9 %collective-permute-start = (bf16[2,1,128,512]{3,2,1,0:T(8,128)(2,1)}, bf16[2,1,128,512]{3,2,1,0:T(8,128)(2,1)S(1)}, u32[]{:S(2)}, u32[]{:S(2)}) collective-permute-start(bf16[2,1,128,512]{3,2,1,0:T(8,128)(2,1)} %get-tuple-element.19), channel_id=1, source_target_pairs={{0,1},{1,2},{2,3},{3,4},{4,5},{5,6},{6,7},{8,9},{9,10},{10,11},{11... | collective-permute-start | bytes 786440 | tf_op jit(solution)/shard_map/ppermute | solution.py:359
  27.8 3.6 %collective-permute-start.1 = (bf16[2,1,128,512]{3,2,1,0:T(8,128)(2,1)}, bf16[2,1,128,512]{3,2,1,0:T(8,128)(2,1)}, u32[]{:S(2)}, u32[]{:S(2)}) collective-permute-start(bf16[2,1,128,512]{3,2,1,0:T(8,128)(2,1)} %get-tuple-element.20), channel_id=1, source_target_pairs={{1,0},{2,1},{3,2},{4,3},{5,4},{6,5},{7,6},{9,8},{10,9},{11,10},{12... | collective-permute-start | bytes 786440 | tf_op jit(solution)/shard_map/ppermute | solution.py:364
  31.4 2.1 %collective-permute-start.5 = (bf16[4,2,128,512]{3,2,1,0:T(8,128)(2,1)}, bf16[4,2,128,512]{3,2,1,0:T(8,128)(2,1)}, u32[]{:S(2)}, u32[]{:S(2)}) collective-permute-start(bf16[4,2,128,512]{3,2,1,0:T(8,128)(2,1)} %get-tuple-element.21.refs_4_.refs_0_), channel_id=1, source_target_pairs={{0,8},{8,16},{16,24},{1,9},{9,17},{17,25},{2,10},{10,18},{18,26},{... | collective-permute-start | bytes 3145736 | tf_op jit(solution)/shard_map/ppermute | solution.py:359
  33.5 2.8 %reshape.11.refs_5_.refs_4_.w_ref.refs_7_.time_ref = bf16[3,512,512]{2,1,0:T(8,128)(2,1)S(1)} reshape(bf16[3,512,2,256]{3,2,1,0:T(2,128)(2,1)} %param.6) | data formatting | bytes 3145728 | tf_op jit(solution)/shard_map/reshape | solution.py:371
  36.3 0.0 copy-start
  36.3 0.0 collective-permute-done.refs_1_
  36.3 0.0 collective-permute-done.1.refs_2_
  36.3 0.0 collective-permute-done.2.refs_5_.refs_1_
  36.3 0.0 copy-start.2
  36.4 2.4 %copy-done.2 = bf16[3,3,512,512]{3,2,1,0:T(8,128)(2,1)S(1)} copy-done((bf16[3,3,512,512]{3,2,1,0:T(8,128)(2,1)S(1)}, bf16[3,3,512,512]{3,2,1,0:T(8,128)(2,1)}, u32[]{:S(2)}) %copy-start.2) | copy-done | bytes 4718616
  38.8 9.9 %hidden_rest.1 = (bf16[2,2,128,512]{3,2,1,0:T(8,128)(2,1)S(1)}, bf16[3,2,128,512]{3,2,1,0:T(8,128)(2,1)S(1)}, bf16[1,2,128,512]{3,2,1,0:T(8,128)(2,1)S(1)}) custom-call(bf16[2,16,128,512]{3,2,1,0:T(8,128)(2,1)} %refs_0_.7, bf16[2,1,128,512]{3,2,1,0:T(8,128)(2,1)S(1)} %collective-permute-done.refs_1_, ...), custom_call_target="tpu_custom_call" | custom-call | flops 7247757312 | bytes 1024 | tf_op jit(solution)/shard_map/hidden_rest/pallas_call | solution.py:290
  48.7 1.9 %collective-permute-start.7 = (bf16[2,2,128,512]{3,2,1,0:T(8,128)(2,1)S(1)}, bf16[2,2,128,512]{3,2,1,0:T(8,128)(2,1)S(1)}, u32[]{:S(2)}, u32[]{:S(2)}) collective-permute-start(bf16[2,2,128,512]{3,2,1,0:T(8,128)(2,1)S(1)} %get-tuple-element.24.refs_6_.own_ref), channel_id=1, source_target_pairs={{0,8},{8,16},{16,24},{1,9},{9,17},{17,25},{2,10},{10,18},{18,26},{... | collective-permute-start | bytes 1572872 | tf_op jit(solution)/shard_map/ppermute | solution.py:359
  50.7 2.1 %collective-permute-start.4 = (bf16[3,2,128,512]{3,2,1,0:T(8,128)(2,1)S(1)}, bf16[3,2,128,512]{3,2,1,0:T(8,128)(2,1)S(1)}, u32[]{:S(2)}, u32[]{:S(2)}) collective-permute-start(bf16[3,2,128,512]{3,2,1,0:T(8,128)(2,1)S(1)} %get-tuple-element.23.refs_0_), channel_id=1, source_target_pairs={{0,8},{8,16},{16,24},{1,9},{9,17},{17,25},{2,10},{10,18},{18,26},{... | collective-permute-start | bytes 2359304 | tf_op jit(solution)/shard_map/ppermute | solution.py:359
  52.8 0.0 collective-permute-done.6.refs_3_
  52.8 0.0 copy-done
  52.8 8.4 %out_2_5.1 = (bf16[4,16,128,256]{3,2,1,0:T(8,128)(2,1)}, bf16[2,4,128,256]{3,2,1,0:T(8,128)(2,1)S(1)}, bf16[2,4,128,256]{3,2,1,0:T(8,128)(2,1)S(1)}) custom-call(bf16[2,2,128,512]{3,2,1,0:T(8,128)(2,1)S(1)} %hidden_1_2.1.refs_2_.refs_0_, bf16[2,2,128,512]{3,2,1,0:T(8,128)(2,1)} %collective-permute-done.2.refs_5_.refs_1_, ...), custom_call_target="tpu_custom_call" | custom-call | flops 4831838208 | bytes 1024 | tf_op jit(solution)/shard_map/out_2_5/pallas_call | solution.py:290
  61.2 6.5 %collective-permute-done.5.refs_1_ = bf16[4,2,128,512]{3,2,1,0:T(8,128)(2,1)} collective-permute-done((bf16[4,2,128,512]{3,2,1,0:T(8,128)(2,1)}, bf16[4,2,128,512]{3,2,1,0:T(8,128)(2,1)}, u32[]{:S(2)}, u32[]{:S(2)}) %collective-permute-start.5) | collective-permute-done | bytes 1048608 | tf_op jit(solution)/shard_map/ppermute | solution.py:359
  67.7 7.5 %out_6_9.1 = (bf16[4,16,128,256]{3,2,1,0:T(8,128)(2,1)}, bf16[2,4,128,256]{3,2,1,0:T(8,128)(2,1)S(1)}) custom-call(bf16[4,2,128,512]{3,2,1,0:T(8,128)(2,1)} %get-tuple-element.21.refs_4_.refs_0_, bf16[4,2,128,512]{3,2,1,0:T(8,128)(2,1)} %collective-permute-done.5.refs_1_, ...), custom_call_target="tpu_custom_call", output_to_operand_aliasing={{0}: (5, {})} | custom-call | flops 4026531840 | bytes 1024 | tf_op jit(solution)/shard_map/out_6_9/pallas_call | solution.py:290
  75.2 3.7 %collective-permute-done.7.prev_ref = bf16[2,2,128,512]{3,2,1,0:T(8,128)(2,1)S(1)} collective-permute-done((bf16[2,2,128,512]{3,2,1,0:T(8,128)(2,1)S(1)}, bf16[2,2,128,512]{3,2,1,0:T(8,128)(2,1)S(1)}, u32[]{:S(2)}, u32[]{:S(2)}) %collective-permute-start.7) | collective-permute-done | bytes 524320 | tf_op jit(solution)/shard_map/ppermute | solution.py:359
  78.9 1.0 up_edges.1.refs_1_.refs_3_
  79.9 1.9 %collective-permute-start.9 = (bf16[1,4,128,256]{3,2,1,0:T(8,128)(2,1)S(1)}, bf16[1,4,128,256]{3,2,1,0:T(8,128)(2,1)S(1)}, u32[]{:S(2)}, u32[]{:S(2)}) collective-permute-start(bf16[1,4,128,256]{3,2,1,0:T(8,128)(2,1)S(1)} %get-tuple-element.33), channel_id=1, source_target_pairs={{0,1},{1,2},{2,3},{3,4},{4,5},{5,6},{6,7},{8,9},{9,10},{10,11},{11... | collective-permute-start | bytes 786440 | tf_op jit(solution)/shard_map/ppermute | solution.py:359
  81.8 3.6 %collective-permute-start.8 = (bf16[1,4,128,256]{3,2,1,0:T(8,128)(2,1)S(1)}, bf16[1,4,128,256]{3,2,1,0:T(8,128)(2,1)S(1)}, u32[]{:S(2)}, u32[]{:S(2)}) collective-permute-start(bf16[1,4,128,256]{3,2,1,0:T(8,128)(2,1)S(1)} %get-tuple-element.34), channel_id=1, source_target_pairs={{1,0},{2,1},{3,2},{4,3},{5,4},{6,5},{7,6},{9,8},{10,9},{11,10},{12... | collective-permute-start | bytes 786440 | tf_op jit(solution)/shard_map/ppermute | solution.py:364
  85.5 2.9 %collective-permute-start.3 = (bf16[1,2,128,512]{3,2,1,0:T(8,128)(2,1)S(1)}, bf16[1,2,128,512]{3,2,1,0:T(8,128)(2,1)S(1)}, u32[]{:S(2)}, u32[]{:S(2)}) collective-permute-start(bf16[1,2,128,512]{3,2,1,0:T(8,128)(2,1)S(1)} %get-tuple-element.22.refs_5_), channel_id=1, source_target_pairs={{0,8},{8,16},{16,24},{1,9},{9,17},{17,25},{2,10},{10,18},{18,26},{... | collective-permute-start | bytes 786440 | tf_op jit(solution)/shard_map/ppermute | solution.py:359
  88.4 0.0 collective-permute-done.9.refs_2_
  88.4 2.3 %out_0_1.1.refs_8_ = bf16[4,16,128,256]{3,2,1,0:T(8,128)(2,1)} custom-call(bf16[2,4,128,256]{3,2,1,0:T(8,128)(2,1)S(1)} %get-tuple-element.28.refs_0_, bf16[2,4,128,256]{3,2,1,0:T(8,128)(2,1)S(1)} %up_edges.1.refs_1_.refs_3_, bf16[1,4,128,256]{3,2,1,0:T(8,128)(2,1)S(1)} %collective-permute-done.9.refs_2_, ...), custom_call_target="tpu_custom_call", output_to_operand_aliasing={{}: (4, {})} | custom-call | flops 1207959552 | bytes 1024 | tf_op jit(solution)/shard_map/out_0_1/pallas_call | solution.py:290
  90.7 0.0 collective-permute-done.8.refs_4_
  90.7 5.0 %collective-permute-done.4.refs_1_ = bf16[3,2,128,512]{3,2,1,0:T(8,128)(2,1)S(1)} collective-permute-done((bf16[3,2,128,512]{3,2,1,0:T(8,128)(2,1)S(1)}, bf16[3,2,128,512]{3,2,1,0:T(8,128)(2,1)S(1)}, u32[]{:S(2)}, u32[]{:S(2)}) %collective-permute-start.4) | collective-permute-done | bytes 786464 | tf_op jit(solution)/shard_map/ppermute | solution.py:359
  95.7 4.9 %out_10_15.1 = (bf16[4,16,128,256]{3,2,1,0:T(8,128)(2,1)}, f32[3,4,128,256]{3,2,1,0:T(8,128)S(1)}, f32[2,128,512]{2,1,0:T(8,128)S(1)}) custom-call(bf16[3,2,128,512]{3,2,1,0:T(8,128)(2,1)S(1)} %get-tuple-element.23.refs_0_, bf16[3,2,128,512]{3,2,1,0:T(8,128)(2,1)S(1)} %collective-permute-done.4.refs_1_, ...), custom_call_target="tpu_custom_call", output_to_operand_aliasing={{0}: (8, {})} | custom-call | flops 3019898880 | bytes 1024 | tf_op jit(solution)/shard_map/out_10_15/pallas_call | solution.py:290
  100.6 0.0 collective-permute-done.3.pair_ref
  100.6 1.9 %out_12_14.1 = bf16[4,16,128,256]{3,2,1,0:T(8,128)(2,1)} custom-call(bf16[1,2,128,512]{3,2,1,0:T(8,128)(2,1)S(1)} %collective-permute-done.3.pair_ref, f32[2,128,512]{2,1,0:T(8,128)S(1)} %get-tuple-element.30.own_ref, f32[3,4,128,256]{3,2,1,0:T(8,128)S(1)} %get-tuple-element.31.part_ref, ...), custom_call_target="tpu_custom_call", output_to_operand_aliasing={{}: (5, {})} | custom-call | flops 872415232 | bytes 1024 | tf_op jit(solution)/shard_map/out_12_14/pallas_call | solution.py:337
  (1 shorter events, 0.0 us)
Async XLA Ops:
  0.0 8.6 %copy-start.1 = (bf16[3,3,512,512]{3,2,1,0:T(8,128)(2,1)S(1)}, bf16[3,3,512,512]{3,2,1,0:T(8,128)(2,1)}, u32[]{:S(2)}) copy-start(bf16[3,3,512,512]{3,2,1,0:T(8,128)(2,1)} %param.5) | copy-start | bytes 14155780
  5.2 31.1 %collective-permute-start.2 = (bf16[2,2,128,512]{3,2,1,0:T(8,128)(2,1)S(1)}, bf16[2,2,128,512]{3,2,1,0:T(8,128)(2,1)}, u32[]{:S(2)}, u32[]{:S(2)}) collective-permute-start(bf16[2,2,128,512]{3,2,1,0:T(8,128)(2,1)S(1)} %hidden_1_2.1.refs_2_.refs_0_), channel_id=1, source_target_pairs={{0,8},{8,16},{16,24},{1,9},{9,17},{17,25},{2,10},{10,18},{18,26},{... | collective-permute-start | bytes 1572872 | tf_op jit(solution)/shard_map/ppermute | solution.py:359
  15.7 37.1 %collective-permute-start.6 = (bf16[4,2,128,512]{3,2,1,0:T(8,128)(2,1)S(1)}, bf16[4,2,128,512]{3,2,1,0:T(8,128)(2,1)}, u32[]{:S(2)}, u32[]{:S(2)}) collective-permute-start(bf16[4,2,128,512]{3,2,1,0:T(8,128)(2,1)S(1)} %hidden_3_6.1.refs_2_), channel_id=1, source_target_pairs={{0,8},{8,16},{16,24},{1,9},{9,17},{17,25},{2,10},{10,18},{18,26},{... | collective-permute-start | bytes 3145736 | tf_op jit(solution)/shard_map/ppermute | solution.py:359
  25.8 10.5 %collective-permute-start = (bf16[2,1,128,512]{3,2,1,0:T(8,128)(2,1)}, bf16[2,1,128,512]{3,2,1,0:T(8,128)(2,1)S(1)}, u32[]{:S(2)}, u32[]{:S(2)}) collective-permute-start(bf16[2,1,128,512]{3,2,1,0:T(8,128)(2,1)} %get-tuple-element.19), channel_id=1, source_target_pairs={{0,1},{1,2},{2,3},{3,4},{4,5},{5,6},{6,7},{8,9},{9,10},{10,11},{11... | collective-permute-start | bytes 786440 | tf_op jit(solution)/shard_map/ppermute | solution.py:359
  27.8 8.6 %collective-permute-start.1 = (bf16[2,1,128,512]{3,2,1,0:T(8,128)(2,1)}, bf16[2,1,128,512]{3,2,1,0:T(8,128)(2,1)}, u32[]{:S(2)}, u32[]{:S(2)}) collective-permute-start(bf16[2,1,128,512]{3,2,1,0:T(8,128)(2,1)} %get-tuple-element.20), channel_id=1, source_target_pairs={{1,0},{2,1},{3,2},{4,3},{5,4},{6,5},{7,6},{9,8},{10,9},{11,10},{12... | collective-permute-start | bytes 786440 | tf_op jit(solution)/shard_map/ppermute | solution.py:364
  31.4 36.3 %collective-permute-start.5 = (bf16[4,2,128,512]{3,2,1,0:T(8,128)(2,1)}, bf16[4,2,128,512]{3,2,1,0:T(8,128)(2,1)}, u32[]{:S(2)}, u32[]{:S(2)}) collective-permute-start(bf16[4,2,128,512]{3,2,1,0:T(8,128)(2,1)} %get-tuple-element.21.refs_4_.refs_0_), channel_id=1, source_target_pairs={{0,8},{8,16},{16,24},{1,9},{9,17},{17,25},{2,10},{10,18},{18,26},{... | collective-permute-start | bytes 3145736 | tf_op jit(solution)/shard_map/ppermute | solution.py:359
  36.3 16.5 %copy-start = (bf16[3,3,256,256]{3,2,1,0:T(8,128)(2,1)S(1)}, bf16[3,3,256,256]{3,2,1,0:T(8,128)(2,1)}, u32[]{:S(2)}) copy-start(bf16[3,3,256,256]{3,2,1,0:T(8,128)(2,1)} %param.7) | copy-start | bytes 3538948
  36.3 2.4 %copy-start.2 = (bf16[3,3,512,512]{3,2,1,0:T(8,128)(2,1)S(1)}, bf16[3,3,512,512]{3,2,1,0:T(8,128)(2,1)}, u32[]{:S(2)}) copy-start(bf16[3,3,512,512]{3,2,1,0:T(8,128)(2,1)} %param.5) | copy-start | bytes 14155780
  48.7 30.1 %collective-permute-start.7 = (bf16[2,2,128,512]{3,2,1,0:T(8,128)(2,1)S(1)}, bf16[2,2,128,512]{3,2,1,0:T(8,128)(2,1)S(1)}, u32[]{:S(2)}, u32[]{:S(2)}) collective-permute-start(bf16[2,2,128,512]{3,2,1,0:T(8,128)(2,1)S(1)} %get-tuple-element.24.refs_6_.own_ref), channel_id=1, source_target_pairs={{0,8},{8,16},{16,24},{1,9},{9,17},{17,25},{2,10},{10,18},{18,26},{... | collective-permute-start | bytes 1572872 | tf_op jit(solution)/shard_map/ppermute | solution.py:359
  50.7 45.1 %collective-permute-start.4 = (bf16[3,2,128,512]{3,2,1,0:T(8,128)(2,1)S(1)}, bf16[3,2,128,512]{3,2,1,0:T(8,128)(2,1)S(1)}, u32[]{:S(2)}, u32[]{:S(2)}) collective-permute-start(bf16[3,2,128,512]{3,2,1,0:T(8,128)(2,1)S(1)} %get-tuple-element.23.refs_0_), channel_id=1, source_target_pairs={{0,8},{8,16},{16,24},{1,9},{9,17},{17,25},{2,10},{10,18},{18,26},{... | collective-permute-start | bytes 2359304 | tf_op jit(solution)/shard_map/ppermute | solution.py:359
  79.9 8.5 %collective-permute-start.9 = (bf16[1,4,128,256]{3,2,1,0:T(8,128)(2,1)S(1)}, bf16[1,4,128,256]{3,2,1,0:T(8,128)(2,1)S(1)}, u32[]{:S(2)}, u32[]{:S(2)}) collective-permute-start(bf16[1,4,128,256]{3,2,1,0:T(8,128)(2,1)S(1)} %get-tuple-element.33), channel_id=1, source_target_pairs={{0,1},{1,2},{2,3},{3,4},{4,5},{5,6},{6,7},{8,9},{9,10},{10,11},{11... | collective-permute-start | bytes 786440 | tf_op jit(solution)/shard_map/ppermute | solution.py:359
  81.8 8.9 %collective-permute-start.8 = (bf16[1,4,128,256]{3,2,1,0:T(8,128)(2,1)S(1)}, bf16[1,4,128,256]{3,2,1,0:T(8,128)(2,1)S(1)}, u32[]{:S(2)}, u32[]{:S(2)}) collective-permute-start(bf16[1,4,128,256]{3,2,1,0:T(8,128)(2,1)S(1)} %get-tuple-element.34), channel_id=1, source_target_pairs={{1,0},{2,1},{3,2},{4,3},{5,4},{6,5},{7,6},{9,8},{10,9},{11,10},{12... | collective-permute-start | bytes 786440 | tf_op jit(solution)/shard_map/ppermute | solution.py:364
  85.5 15.2 %collective-permute-start.3 = (bf16[1,2,128,512]{3,2,1,0:T(8,128)(2,1)S(1)}, bf16[1,2,128,512]{3,2,1,0:T(8,128)(2,1)S(1)}, u32[]{:S(2)}, u32[]{:S(2)}) collective-permute-start(bf16[1,2,128,512]{3,2,1,0:T(8,128)(2,1)S(1)} %get-tuple-element.22.refs_5_), channel_id=1, source_target_pairs={{0,8},{8,16},{16,24},{1,9},{9,17},{17,25},{2,10},{10,18},{18,26},{... | collective-permute-start | bytes 786440 | tf_op jit(solution)/shard_map/ppermute | solution.py:359

commit v2 on v1

--- a/solution.py
+++ b/solution.py
@@ -75,19 +75,23 @@
             )
 
 
-def lift_own(own_ref, time_ref, out_ref):
-    first, second = own_ref[0, 0], own_ref[0, 1]
-    out_ref[0] = jnp.dot(first, time_ref[2], preferred_element_type=jnp.float32)
-    out_ref[1] = jnp.dot(first, time_ref[1], preferred_element_type=jnp.float32) + jnp.dot(
-        second, time_ref[2], preferred_element_type=jnp.float32
-    )
+def lift_own(own_ref, start, count, time_ref, out_ref, at):
+    _, _, width, channels = own_ref.shape
+    size = count * width
+    first, second = [own_ref[start : start + count, frame].reshape(size, channels) for frame in range(2)]
+    shape = (count,) + out_ref.shape[2:]
+    total = jnp.dot(first, time_ref[2], preferred_element_type=jnp.float32)
+    out_ref[at : at + count, 0] = total.reshape(shape)
+    total = jnp.dot(first, time_ref[1], preferred_element_type=jnp.float32)
+    total += jnp.dot(second, time_ref[2], preferred_element_type=jnp.float32)
+    out_ref[at : at + count, 1] = total.reshape(shape)
 
 
 def stage_kernel(plan, *refs):
     refs = list(refs)
     sources = [refs.pop(0) for _ in range(plan["sources"])]
     w_ref = refs.pop(0)
-    time_ref = refs.pop(0) if plan["lifts"] else None
+    time_ref = refs.pop(0) if plan["lifts"] or plan["own_parts"] else None
     for _ in range(plan["unread"]):
         refs.pop(0)
     outs = [refs.pop(0) for _ in range(plan["outs"])]
@@ -166,9 +170,8 @@
             if residual is not None:
                 total += x_ref[residual].reshape(size, x_ref.shape[3]).astype(jnp.float32)
             outs[out][index] = total.reshape(x_ref.shape[1:])
-        if plan["own_part"] is not None:
-            source, out = plan["own_part"]
-            lift_own(sources[source], time_ref, outs[out])
+        for source, start, count, out, at in plan["own_parts"]:
+            lift_own(sources[source], start, count, time_ref, outs[out], at)
 
     target = 0
     for number, (source, count, active, out, start) in enumerate(plan["runs"]):
@@ -237,14 +240,14 @@
     fetch=False,
     prepared=(),
     partials=(),
-    own_part=None,
+    own_parts=(),
 ):
     frames, width, channels = dims
     rows_in = max(target + count for *_, count, target in list(loads) + list(lifts))
     rows_out = sum(run[1] for run in runs)
     args = list(sources) + [weight]
     spaces = [pl.ANY if fetched else pltpu.VMEM] * len(sources) + [pltpu.HBM if fetch else pltpu.VMEM]
-    if lifts:
+    if lifts or own_parts:
         args.append(time)
         spaces.append(pltpu.VMEM)
     unread = list(after) + ([] if into is None else [into])
@@ -266,9 +269,9 @@
         fetch=fetch,
         prepared=prepared,
         partials=partials,
-        own_part=own_part,
-    )
-    in_float = {entry[0] for entry in partials} | ({own_part[1]} if own_part else set())
+        own_parts=own_parts,
+    )
+    in_float = {entry[0] for entry in partials} | {entry[3] for entry in own_parts}
     scratch = [
         pltpu.VMEM((rows_in, frames, width, channels), jnp.bfloat16),
         pltpu.VMEM((rows_in, frames, width, 3 * channels), jnp.bfloat16),
@@ -303,11 +306,16 @@
     )(*args)
 
 
-def finish_kernel(pair_ref, own_ref, part_ref, time_ref, w_ref, _, out_ref, x_ref, act_ref, stage_ref, sem, *, start):
-    frames, width, channels = x_ref.shape[1:]
-    before, latest = pair_ref[0, 0], pair_ref[0, 1]
+def arrive_kernel(plan, *refs):
+    pair_ref, own_ref, part_ref, time_ref, w_ref, _, out_ref = refs[:7]
+    refs = list(refs[7:])
+    later_ref = refs.pop(0) if plan["later"] else None
+    x_ref, act_ref, stage_ref, sem = refs
+    count, frames, width, channels = x_ref.shape
+    depth = pair_ref.shape[3]
+    before, latest = [pair_ref[:, frame].reshape(count * width, depth) for frame in range(2)]
     for pair in range(2):
-        total = own_ref[pair]
+        total = own_ref[plan["own_at"] : plan["own_at"] + count, pair].reshape(count * width, 2 * channels)
         if pair == 0:
             total += jnp.dot(before, time_ref[0], preferred_element_type=jnp.float32)
             total += jnp.dot(latest, time_ref[1], preferred_element_type=jnp.float32)
@@ -315,40 +323,59 @@
             total += jnp.dot(latest, time_ref[0], preferred_element_type=jnp.float32)
         total = total.astype(jnp.bfloat16)
         for half in range(2):
-            x_ref[0, 2 * pair + half] = total[:, half * channels : (half + 1) * channels]
-            activate(x_ref, act_ref, 0, 2 * pair + half)
+            x_ref[:, 2 * pair + half] = total[:, half * channels : (half + 1) * channels].reshape(
+                count, width, channels
+            )
+            for row in range(count):
+                activate(x_ref, act_ref, row, 2 * pair + half)
     copies = []
-    for row in range(3):
-        total = jnp.dot(
-            act_ref[0].reshape(frames * width, 3 * channels), w_ref[2 - row], preferred_element_type=jnp.float32
-        ).reshape(frames, width, channels)
-        total += part_ref[row]
-        if row == 1:
-            total += x_ref[0].astype(jnp.float32)
-        stage_ref[row] = total.astype(jnp.bfloat16)
-        copies.append(pltpu.make_async_copy(stage_ref.at[row], out_ref.at[:, start + row], sem.at[row]))
+    for later, index, part, residual, taps in plan["terms"]:
+        total = None
+        for tap, row in taps:
+            lhs = act_ref[row].reshape(frames * width, 3 * channels)
+            value = jnp.dot(lhs, w_ref[tap], preferred_element_type=jnp.float32)
+            total = value if total is None else total + value
+        total = total.reshape(frames, width, channels)
+        if part is not None:
+            total += part_ref[part]
+        if residual is not None:
+            total += x_ref[residual].astype(jnp.float32)
+        if later:
+            later_ref[index] = total
+            continue
+        place = len(copies)
+        stage_ref[place] = total.astype(jnp.bfloat16)
+        copies.append(pltpu.make_async_copy(stage_ref.at[place], out_ref.at[:, index], sem.at[place]))
         copies[-1].start()
     for copy in copies:
         copy.wait()
 
 
-def finish(name, pair, own, part, time, weight, into, start):
-    rows, frames, width, channels = part.shape
+def arrive(name, pair, own, own_at, part, time, weight, into, terms):
+    count = pair.shape[0]
+    _, frames, width, channels = part.shape
+    later = sum(term[0] for term in terms)
+    final = len(terms) - later
+    shapes = [jax.ShapeDtypeStruct(into.shape, into.dtype)]
+    if later:
+        shapes.append(jax.ShapeDtypeStruct((later,) + part.shape[1:], jnp.float32))
     return pl.pallas_call(
-        functools.partial(finish_kernel, start=start),
-        out_shape=jax.ShapeDtypeStruct(into.shape, into.dtype),
+        functools.partial(arrive_kernel, dict(terms=terms, own_at=own_at, later=later)),
+        out_shape=shapes,
         in_specs=[pl.BlockSpec(memory_space=pltpu.VMEM)] * 5 + [pl.BlockSpec(memory_space=pl.ANY)],
-        out_specs=pl.BlockSpec(memory_space=pltpu.HBM),
+        out_specs=[pl.BlockSpec(memory_space=pltpu.HBM)] + [pl.BlockSpec(memory_space=pltpu.VMEM)] * (len(shapes) - 1),
         scratch_shapes=[
-            pltpu.VMEM((1, frames, width, channels), jnp.bfloat16),
-            pltpu.VMEM((1, frames, width, 3 * channels), jnp.bfloat16),
-            pltpu.VMEM((rows, frames, width, channels), jnp.bfloat16),
-            pltpu.SemaphoreType.DMA((rows,)),
+            pltpu.VMEM((count, frames, width, channels), jnp.bfloat16),
+            pltpu.VMEM((count, frames, width, 3 * channels), jnp.bfloat16),
+            pltpu.VMEM((final, frames, width, channels), jnp.bfloat16),
+            pltpu.SemaphoreType.DMA((final,)),
         ],
         input_output_aliases={5: 0},
-        compiler_params=pltpu.CompilerParams(vmem_limit_bytes=12 * MIB),
+        compiler_params=pltpu.CompilerParams(vmem_limit_bytes=16 * MIB),
         cost_estimate=pl.CostEstimate(
-            flops=2 * frames * width * channels * (9 * channels + 2 * time.shape[1]), bytes_accessed=1024, transcendentals=0
+            flops=2 * frames * width * channels * (3 * len(terms) * channels + 2 * count * time.shape[1]),
+            bytes_accessed=1024,
+            transcendentals=0,
         ),
         name=name,
     )(pair, own, part, time, weight, into)
@@ -460,37 +487,60 @@
     ud = upsample("up_edges", hd, pd, time, depth, uc)
     up_above = to_next(ud[:1], "rows")
     up_below = to_previous(ud[1:], "rows")
-    (out,) = stage(
+    out, part, own = stage(
         "out_0_1",
-        [ua, ud, up_above],
+        [ua, ud, up_above, uc, up_below, he, hf],
         out_w,
-        [(2, 0, 1, 0), (1, 1, 1, 1), (0, 0, 2, 2)],
+        [(2, 0, 1, 0), (1, 1, 1, 1), (0, 0, 2, 2), (3, 0, 2, 4), (1, 0, 1, 6), (4, 0, 1, 7)],
         [(0, 2, 0, 0, 0)],
-        [whole],
+        [whole, (4,) + lifted(1)[1:], (4, 2, width, 2 * depth)],
         fine,
         staged=True,
         into=out,
-    )
-    out, part, own_part = stage(
+        time=time,
+        prepared=(4, 5, 6, 7),
+        partials=[
+            (1, 0, 5, ((0, 4), (1, 5))),
+            (1, 1, None, ((0, 5),)),
+            (1, 2, None, ((2, 6),)),
+            (1, 3, 6, ((1, 6), (2, 7))),
+        ],
+        own_parts=[(5, 0, 3, 2, 0), (6, 0, 1, 2, 3)],
+    )
+    out, last_part = arrive(
         "out_10_15",
-        [he, pe, uc, ud, up_below, hf],
+        pe,
+        own,
+        0,
+        part,
+        time,
         out_w,
-        [(2, 0, 2, 0), (3, 0, 1, 5), (4, 0, 1, 6)],
-        [(0, 2, 0, 0, 10), (4, 1, 0, 0, 15)],
-        [whole, (3,) + lifted(1)[1:], (2, width, 2 * depth)],
-        fine,
-        staged=True,
-        lifts=[(0, 1, 0, 2, 2), (0, 1, 2, 1, 4)],
-        time=time,
-        into=out,
-        partials=[
-            (1, 0, 3, ((0, 2), (1, 3))),
-            (1, 1, None, ((0, 3), (2, 4))),
-            (1, 2, 4, ((1, 4), (2, 5))),
+        out,
+        [
+            (False, 10, 0, None, ((2, 0),)),
+            (False, 11, 1, 0, ((1, 0), (2, 1))),
+            (False, 15, 3, None, ((0, 2),)),
+            (True, 0, None, 1, ((0, 0), (1, 1))),
+            (True, 1, None, None, ((0, 1), (2, 2))),
+            (True, 2, 2, 2, ((1, 2),)),
         ],
-        own_part=(5, 2),
-    )
-    return finish("out_12_14", pf, own_part, part, time, out_w, out, 12)
+    )
+    (out,) = arrive(
+        "out_12_14",
+        pf,
+        own,
+        3,
+        last_part,
+        time,
+        out_w,
+        out,
+        [
+            (False, 12, 0, None, ((2, 0),)),
+            (False, 13, 1, 0, ((1, 0),)),
+            (False, 14, 2, None, ((0, 0),)),
+        ],
+    )
+    return out
 
 
 def upsample_kernel(own_ref, prev_ref, w_ref, _, out_ref):

time: 103 us -> 103 us (level)
    pallas_call x8 -> x7, Pallas kernels: 53.4 us -> 50.4 us  [stage(): pl.pallas_call(functools.partial(stage_kernel, plan), out_shape=[jax.Shap...]
    pallas_call x1 -> x2, Pallas kernels: 1.94 us -> 4.76 us  [arrive(): pl.pallas_call(functools.partial(arrive_kernel, dict(terms=terms, own_at=...]
  transfers between devices with their start and end apart: 10 -> 10, of which waited for: 3 -> 5; matrix products, arithmetic and copies ran while one was open for 3% -> 3% of each run, Pallas kernels for 48% -> 48%
where the time goes in v2:
time: 103 us; the launch traced here: 102 us
  Pallas kernels  56.1 us (54%)
  starting transfers between devices  25.5 us (25%)
  waiting for transfers between devices  15.1 us (15%)
  local copies, waits for them, and re-layouts  5.24 us (5%)
    pallas_call x7, Pallas kernels, stage(): pl.pallas_call(functools.partial(stage_kernel, plan), out_shape=[jax.Shap...  50.4 us
    ppermute x8, starting transfers between devices, to_next(): return lax.ppermute(value, axis, [(i, i + 1) for i in range(count - 1)])  18.2 us
    ppermute x8, waiting for transfers between devices, to_next(): return lax.ppermute(value, axis, [(i, i + 1) for i in range(count - 1)])  14.2 us
    ppermute x2, starting transfers between devices, to_previous(): return lax.ppermute(value, axis, [(i + 1, i) for i in range(count - 1)])  7.29 us
    pallas_call x2, Pallas kernels, arrive(): pl.pallas_call(functools.partial(arrive_kernel, dict(terms=terms, own_at=...  4.76 us
    reshape x1, local copies, waits for them, and re-layouts, on_device(): time = time_weight.reshape(3, channels, 2 * depth)  2.77 us
    unnamed x6, local copies, waits for them, and re-layouts  2.43 us
  transfers between devices with their start and end apart: 10, of which 5 were waited for; matrix products, arithmetic and copies ran while one was open for 3% of the time, Pallas kernels for 48%

profile of v2, /device:TPU:20, one launch (start us, length us, event | category | flops | bytes accessed | tf_op | source)
XLA Modules:
  0.0 102.5 jit_solution(17800600102279990284)
XLA Ops:
  0.0 0.0 copy-start.1
  0.0 5.2 %hidden_1_2.1.refs_2_.refs_0_ = bf16[2,2,128,512]{3,2,1,0:T(8,128)(2,1)S(1)} custom-call(bf16[2,16,128,512]{3,2,1,0:T(8,128)(2,1)} %refs_0_.7, bf16[3,1536,512]{2,1,0:T(8,128)(2,1)} %bitcast.7), custom_call_target="tpu_custom_call" | custom-call | flops 2415919104 | bytes 1024 | tf_op jit(solution)/shard_map/hidden_1_2/pallas_call | solution.py:293
  5.2 3.4 %collective-permute-start.2 = (bf16[2,2,128,512]{3,2,1,0:T(8,128)(2,1)S(1)}, bf16[2,2,128,512]{3,2,1,0:T(8,128)(2,1)}, u32[]{:S(2)}, u32[]{:S(2)}) collective-permute-start(bf16[2,2,128,512]{3,2,1,0:T(8,128)(2,1)S(1)} %hidden_1_2.1.refs_2_.refs_0_), channel_id=1, source_target_pairs={{0,8},{8,16},{16,24},{1,9},{9,17},{17,25},{2,10},{10,18},{18,26},{... | collective-permute-start | bytes 1572872 | tf_op jit(solution)/shard_map/ppermute | solution.py:386
  8.6 0.0 copy-done.1
  8.6 7.1 %hidden_3_6.1.refs_2_ = bf16[4,2,128,512]{3,2,1,0:T(8,128)(2,1)S(1)} custom-call(bf16[2,16,128,512]{3,2,1,0:T(8,128)(2,1)} %refs_0_.7, bf16[3,1536,512]{2,1,0:T(8,128)(2,1)S(1)} %bitcast.8, bf16[2,2,128,512]{3,2,1,0:T(8,128)(2,1)S(1)} %hidden_1_2.1.refs_2_.refs_0_), custom_call_target="tpu_custom_call" | custom-call | flops 4831838208 | bytes 1024 | tf_op jit(solution)/shard_map/hidden_3_6/pallas_call | solution.py:293
  15.7 1.9 %collective-permute-start.4 = (bf16[4,2,128,512]{3,2,1,0:T(8,128)(2,1)S(1)}, bf16[4,2,128,512]{3,2,1,0:T(8,128)(2,1)}, u32[]{:S(2)}, u32[]{:S(2)}) collective-permute-start(bf16[4,2,128,512]{3,2,1,0:T(8,128)(2,1)S(1)} %hidden_3_6.1.refs_2_), channel_id=1, source_target_pairs={{0,8},{8,16},{16,24},{1,9},{9,17},{17,25},{2,10},{10,18},{18,26},{... | collective-permute-start | bytes 3145736 | tf_op jit(solution)/shard_map/ppermute | solution.py:386
  17.6 8.2 %hidden_7_10.1 = (bf16[4,2,128,512]{3,2,1,0:T(8,128)(2,1)}, bf16[2,1,128,512]{3,2,1,0:T(8,128)(2,1)}, bf16[2,1,128,512]{3,2,1,0:T(8,128)(2,1)}) custom-call(bf16[2,16,128,512]{3,2,1,0:T(8,128)(2,1)} %refs_0_.7, bf16[3,1536,512]{2,1,0:T(8,128)(2,1)S(1)} %bitcast.9, bf16[4,2,128,512]{3,2,1,0:T(8,128)(2,1)S(1)} %hidden_3_6.1.refs_2_), custom_call_target="tpu_custom_call" | custom-call | flops 4831838208 | bytes 1024 | tf_op jit(solution)/shard_map/hidden_7_10/pallas_call | solution.py:293
  25.8 1.9 %collective-permute-start = (bf16[2,1,128,512]{3,2,1,0:T(8,128)(2,1)}, bf16[2,1,128,512]{3,2,1,0:T(8,128)(2,1)S(1)}, u32[]{:S(2)}, u32[]{:S(2)}) collective-permute-start(bf16[2,1,128,512]{3,2,1,0:T(8,128)(2,1)} %get-tuple-element.21), channel_id=1, source_target_pairs={{0,1},{1,2},{2,3},{3,4},{4,5},{5,6},{6,7},{8,9},{9,10},{10,11},{11... | collective-permute-start | bytes 786440 | tf_op jit(solution)/shard_map/ppermute | solution.py:386
  27.8 3.6 %collective-permute-start.1 = (bf16[2,1,128,512]{3,2,1,0:T(8,128)(2,1)}, bf16[2,1,128,512]{3,2,1,0:T(8,128)(2,1)}, u32[]{:S(2)}, u32[]{:S(2)}) collective-permute-start(bf16[2,1,128,512]{3,2,1,0:T(8,128)(2,1)} %get-tuple-element.22), channel_id=1, source_target_pairs={{1,0},{2,1},{3,2},{4,3},{5,4},{6,5},{7,6},{9,8},{10,9},{11,10},{12... | collective-permute-start | bytes 786440 | tf_op jit(solution)/shard_map/ppermute | solution.py:391
  31.4 2.1 %collective-permute-start.6 = (bf16[4,2,128,512]{3,2,1,0:T(8,128)(2,1)}, bf16[4,2,128,512]{3,2,1,0:T(8,128)(2,1)}, u32[]{:S(2)}, u32[]{:S(2)}) collective-permute-start(bf16[4,2,128,512]{3,2,1,0:T(8,128)(2,1)} %get-tuple-element.23.refs_4_.refs_0_), channel_id=1, source_target_pairs={{0,8},{8,16},{16,24},{1,9},{9,17},{17,25},{2,10},{10,18},{18,26},{... | collective-permute-start | bytes 3145736 | tf_op jit(solution)/shard_map/ppermute | solution.py:386
  33.5 2.8 %reshape.11.refs_5_.refs_4_.w_ref.refs_8_.refs_3_ = bf16[3,512,512]{2,1,0:T(8,128)(2,1)S(1)} reshape(bf16[3,512,2,256]{3,2,1,0:T(2,128)(2,1)} %param.6) | data formatting | bytes 3145728 | tf_op jit(solution)/shard_map/reshape | solution.py:398
  36.3 0.0 copy-start
  36.3 0.0 collective-permute-done.refs_1_
  36.3 0.0 collective-permute-done.1.refs_2_
  36.3 0.0 collective-permute-done.2.refs_5_.refs_1_
  36.3 0.0 copy-start.2
  36.4 2.4 %copy-done.2 = bf16[3,3,512,512]{3,2,1,0:T(8,128)(2,1)S(1)} copy-done((bf16[3,3,512,512]{3,2,1,0:T(8,128)(2,1)S(1)}, bf16[3,3,512,512]{3,2,1,0:T(8,128)(2,1)}, u32[]{:S(2)}) %copy-start.2) | copy-done | bytes 4718616
  38.8 9.9 %hidden_rest.1 = (bf16[2,2,128,512]{3,2,1,0:T(8,128)(2,1)S(1)}, bf16[3,2,128,512]{3,2,1,0:T(8,128)(2,1)S(1)}, bf16[1,2,128,512]{3,2,1,0:T(8,128)(2,1)S(1)}) custom-call(bf16[2,16,128,512]{3,2,1,0:T(8,128)(2,1)} %refs_0_.7, bf16[2,1,128,512]{3,2,1,0:T(8,128)(2,1)S(1)} %collective-permute-done.refs_1_, ...), custom_call_target="tpu_custom_call" | custom-call | flops 7247757312 | bytes 1024 | tf_op jit(solution)/shard_map/hidden_rest/pallas_call | solution.py:293
  48.7 1.9 %collective-permute-start.5 = (bf16[2,2,128,512]{3,2,1,0:T(8,128)(2,1)S(1)}, bf16[2,2,128,512]{3,2,1,0:T(8,128)(2,1)S(1)}, u32[]{:S(2)}, u32[]{:S(2)}) collective-permute-start(bf16[2,2,128,512]{3,2,1,0:T(8,128)(2,1)S(1)} %get-tuple-element.25.refs_6_.own_ref), channel_id=1, source_target_pairs={{0,8},{8,16},{16,24},{1,9},{9,17},{17,25},{2,10},{10,18},{18,26},{... | collective-permute-start | bytes 1572872 | tf_op jit(solution)/shard_map/ppermute | solution.py:386
  50.6 2.1 %collective-permute-start.9 = (bf16[3,2,128,512]{3,2,1,0:T(8,128)(2,1)S(1)}, bf16[3,2,128,512]{3,2,1,0:T(8,128)(2,1)S(1)}, u32[]{:S(2)}, u32[]{:S(2)}) collective-permute-start(bf16[3,2,128,512]{3,2,1,0:T(8,128)(2,1)S(1)} %get-tuple-element.30.refs_5_), channel_id=1, source_target_pairs={{0,8},{8,16},{16,24},{1,9},{9,17},{17,25},{2,10},{10,18},{18,26},{... | collective-permute-start | bytes 2359304 | tf_op jit(solution)/shard_map/ppermute | solution.py:386
  52.8 0.0 collective-permute-done.4.refs_3_
  52.8 0.0 copy-done
  52.8 8.4 %out_2_5.1 = (bf16[4,16,128,256]{3,2,1,0:T(8,128)(2,1)}, bf16[2,4,128,256]{3,2,1,0:T(8,128)(2,1)S(1)}, bf16[2,4,128,256]{3,2,1,0:T(8,128)(2,1)S(1)}) custom-call(bf16[2,2,128,512]{3,2,1,0:T(8,128)(2,1)S(1)} %hidden_1_2.1.refs_2_.refs_0_, bf16[2,2,128,512]{3,2,1,0:T(8,128)(2,1)} %collective-permute-done.2.refs_5_.refs_1_, ...), custom_call_target="tpu_custom_call" | custom-call | flops 4831838208 | bytes 1024 | tf_op jit(solution)/shard_map/out_2_5/pallas_call | solution.py:293
  61.2 6.5 %collective-permute-done.6.refs_1_ = bf16[4,2,128,512]{3,2,1,0:T(8,128)(2,1)} collective-permute-done((bf16[4,2,128,512]{3,2,1,0:T(8,128)(2,1)}, bf16[4,2,128,512]{3,2,1,0:T(8,128)(2,1)}, u32[]{:S(2)}, u32[]{:S(2)}) %collective-permute-start.6) | collective-permute-done | bytes 1048608 | tf_op jit(solution)/shard_map/ppermute | solution.py:386
  67.7 7.5 %out_6_9.1 = (bf16[4,16,128,256]{3,2,1,0:T(8,128)(2,1)}, bf16[2,4,128,256]{3,2,1,0:T(8,128)(2,1)S(1)}) custom-call(bf16[4,2,128,512]{3,2,1,0:T(8,128)(2,1)} %get-tuple-element.23.refs_4_.refs_0_, bf16[4,2,128,512]{3,2,1,0:T(8,128)(2,1)} %collective-permute-done.6.refs_1_, ...), custom_call_target="tpu_custom_call", output_to_operand_aliasing={{0}: (5, {})} | custom-call | flops 4026531840 | bytes 1024 | tf_op jit(solution)/shard_map/out_6_9/pallas_call | solution.py:293
  75.2 3.7 %collective-permute-done.5.prev_ref = bf16[2,2,128,512]{3,2,1,0:T(8,128)(2,1)S(1)} collective-permute-done((bf16[2,2,128,512]{3,2,1,0:T(8,128)(2,1)S(1)}, bf16[2,2,128,512]{3,2,1,0:T(8,128)(2,1)S(1)}, u32[]{:S(2)}, u32[]{:S(2)}) %collective-permute-start.5) | collective-permute-done | bytes 524320 | tf_op jit(solution)/shard_map/ppermute | solution.py:386
  78.9 1.0 up_edges.1.refs_1_
  79.9 1.9 %collective-permute-start.7 = (bf16[1,4,128,256]{3,2,1,0:T(8,128)(2,1)S(1)}, bf16[1,4,128,256]{3,2,1,0:T(8,128)(2,1)S(1)}, u32[]{:S(2)}, u32[]{:S(2)}) collective-permute-start(bf16[1,4,128,256]{3,2,1,0:T(8,128)(2,1)S(1)} %get-tuple-element.38), channel_id=1, source_target_pairs={{0,1},{1,2},{2,3},{3,4},{4,5},{5,6},{6,7},{8,9},{9,10},{10,11},{11... | collective-permute-start | bytes 786440 | tf_op jit(solution)/shard_map/ppermute | solution.py:386
  81.8 3.6 %collective-permute-start.8 = (bf16[1,4,128,256]{3,2,1,0:T(8,128)(2,1)S(1)}, bf16[1,4,128,256]{3,2,1,0:T(8,128)(2,1)S(1)}, u32[]{:S(2)}, u32[]{:S(2)}) collective-permute-start(bf16[1,4,128,256]{3,2,1,0:T(8,128)(2,1)S(1)} %get-tuple-element.37), channel_id=1, source_target_pairs={{1,0},{2,1},{3,2},{4,3},{5,4},{6,5},{7,6},{9,8},{10,9},{11,10},{12... | collective-permute-start | bytes 786440 | tf_op jit(solution)/shard_map/ppermute | solution.py:391
  85.5 2.9 %collective-permute-start.3 = (bf16[1,2,128,512]{3,2,1,0:T(8,128)(2,1)S(1)}, bf16[1,2,128,512]{3,2,1,0:T(8,128)(2,1)S(1)}, u32[]{:S(2)}, u32[]{:S(2)}) collective-permute-start(bf16[1,2,128,512]{3,2,1,0:T(8,128)(2,1)S(1)} %get-tuple-element.24.refs_6_), channel_id=1, source_target_pairs={{0,8},{8,16},{16,24},{1,9},{9,17},{17,25},{2,10},{10,18},{18,26},{... | collective-permute-start | bytes 786440 | tf_op jit(solution)/shard_map/ppermute | solution.py:386
  88.4 0.0 collective-permute-done.7.refs_2_
  88.4 0.9 collective-permute-done.8.refs_4_
  89.3 4.2 %out_0_1.1 = (bf16[4,16,128,256]{3,2,1,0:T(8,128)(2,1)}, f32[4,4,128,256]{3,2,1,0:T(8,128)S(1)}, f32[4,2,128,512]{3,2,1,0:T(8,128)S(1)}) custom-call(bf16[2,4,128,256]{3,2,1,0:T(8,128)(2,1)S(1)} %get-tuple-element.26.refs_0_, bf16[2,4,128,256]{3,2,1,0:T(8,128)(2,1)S(1)} %up_edges.1.refs_1_, ...), custom_call_target="tpu_custom_call", output_to_operand_aliasing={{0}: (9, {})} | custom-call | flops 1207959552 | bytes 1024 | tf_op jit(solution)/shard_map/out_0_1/pallas_call | solution.py:293
  93.5 2.2 %collective-permute-done.9.refs_0_ = bf16[3,2,128,512]{3,2,1,0:T(8,128)(2,1)S(1)} collective-permute-done((bf16[3,2,128,512]{3,2,1,0:T(8,128)(2,1)S(1)}, bf16[3,2,128,512]{3,2,1,0:T(8,128)(2,1)S(1)}, u32[]{:S(2)}, u32[]{:S(2)}) %collective-permute-start.9) | collective-permute-done | bytes 786464 | tf_op jit(solution)/shard_map/ppermute | solution.py:386
  95.7 2.8 %out_10_15.1 = (bf16[4,16,128,256]{3,2,1,0:T(8,128)(2,1)}, f32[3,4,128,256]{3,2,1,0:T(8,128)S(1)}) custom-call(bf16[3,2,128,512]{3,2,1,0:T(8,128)(2,1)S(1)} %collective-permute-done.9.refs_0_, f32[4,2,128,512]{3,2,1,0:T(8,128)S(1)} %get-tuple-element.32.refs_1_, f32[4,4,128,256]{3,2,1,0:T(8,128)S(1)} %get-tuple-element.33.refs_2_, ...), custom_call_target="tpu_custom_call", output_to_operand_aliasing={{0}: (5, {})} | custom-call | flops 2013265920 | bytes 1024 | tf_op jit(solution)/shard_map/out_10_15/pallas_call | solution.py:362
  98.5 1.8 %collective-permute-done.3.refs_0_ = bf16[1,2,128,512]{3,2,1,0:T(8,128)(2,1)S(1)} collective-permute-done((bf16[1,2,128,512]{3,2,1,0:T(8,128)(2,1)S(1)}, bf16[1,2,128,512]{3,2,1,0:T(8,128)(2,1)S(1)}, u32[]{:S(2)}, u32[]{:S(2)}) %collective-permute-start.3) | collective-permute-done | bytes 262176 | tf_op jit(solution)/shard_map/ppermute | solution.py:386
  100.3 1.9 %out_12_14.1 = bf16[4,16,128,256]{3,2,1,0:T(8,128)(2,1)} custom-call(bf16[1,2,128,512]{3,2,1,0:T(8,128)(2,1)S(1)} %collective-permute-done.3.refs_0_, f32[4,2,128,512]{3,2,1,0:T(8,128)S(1)} %get-tuple-element.32.refs_1_, f32[3,4,128,256]{3,2,1,0:T(8,128)S(1)} %get-tuple-element.35.refs_2_, ...), custom_call_target="tpu_custom_call", output_to_operand_aliasing={{}: (5, {})} | custom-call | flops 872415232 | bytes 1024 | tf_op jit(solution)/shard_map/out_12_14/pallas_call | solution.py:362
  (1 shorter events, 0.0 us)
Async XLA Ops:
  0.0 8.6 %copy-start.1 = (bf16[3,3,512,512]{3,2,1,0:T(8,128)(2,1)S(1)}, bf16[3,3,512,512]{3,2,1,0:T(8,128)(2,1)}, u32[]{:S(2)}) copy-start(bf16[3,3,512,512]{3,2,1,0:T(8,128)(2,1)} %param.5) | copy-start | bytes 14155780
  5.2 31.1 %collective-permute-start.2 = (bf16[2,2,128,512]{3,2,1,0:T(8,128)(2,1)S(1)}, bf16[2,2,128,512]{3,2,1,0:T(8,128)(2,1)}, u32[]{:S(2)}, u32[]{:S(2)}) collective-permute-start(bf16[2,2,128,512]{3,2,1,0:T(8,128)(2,1)S(1)} %hidden_1_2.1.refs_2_.refs_0_), channel_id=1, source_target_pairs={{0,8},{8,16},{16,24},{1,9},{9,17},{17,25},{2,10},{10,18},{18,26},{... | collective-permute-start | bytes 1572872 | tf_op jit(solution)/shard_map/ppermute | solution.py:386
  15.7 37.1 %collective-permute-start.4 = (bf16[4,2,128,512]{3,2,1,0:T(8,128)(2,1)S(1)}, bf16[4,2,128,512]{3,2,1,0:T(8,128)(2,1)}, u32[]{:S(2)}, u32[]{:S(2)}) collective-permute-start(bf16[4,2,128,512]{3,2,1,0:T(8,128)(2,1)S(1)} %hidden_3_6.1.refs_2_), channel_id=1, source_target_pairs={{0,8},{8,16},{16,24},{1,9},{9,17},{17,25},{2,10},{10,18},{18,26},{... | collective-permute-start | bytes 3145736 | tf_op jit(solution)/shard_map/ppermute | solution.py:386
  25.8 10.5 %collective-permute-start = (bf16[2,1,128,512]{3,2,1,0:T(8,128)(2,1)}, bf16[2,1,128,512]{3,2,1,0:T(8,128)(2,1)S(1)}, u32[]{:S(2)}, u32[]{:S(2)}) collective-permute-start(bf16[2,1,128,512]{3,2,1,0:T(8,128)(2,1)} %get-tuple-element.21), channel_id=1, source_target_pairs={{0,1},{1,2},{2,3},{3,4},{4,5},{5,6},{6,7},{8,9},{9,10},{10,11},{11... | collective-permute-start | bytes 786440 | tf_op jit(solution)/shard_map/ppermute | solution.py:386
  27.8 8.6 %collective-permute-start.1 = (bf16[2,1,128,512]{3,2,1,0:T(8,128)(2,1)}, bf16[2,1,128,512]{3,2,1,0:T(8,128)(2,1)}, u32[]{:S(2)}, u32[]{:S(2)}) collective-permute-start(bf16[2,1,128,512]{3,2,1,0:T(8,128)(2,1)} %get-tuple-element.22), channel_id=1, source_target_pairs={{1,0},{2,1},{3,2},{4,3},{5,4},{6,5},{7,6},{9,8},{10,9},{11,10},{12... | collective-permute-start | bytes 786440 | tf_op jit(solution)/shard_map/ppermute | solution.py:391
  31.4 36.3 %collective-permute-start.6 = (bf16[4,2,128,512]{3,2,1,0:T(8,128)(2,1)}, bf16[4,2,128,512]{3,2,1,0:T(8,128)(2,1)}, u32[]{:S(2)}, u32[]{:S(2)}) collective-permute-start(bf16[4,2,128,512]{3,2,1,0:T(8,128)(2,1)} %get-tuple-element.23.refs_4_.refs_0_), channel_id=1, source_target_pairs={{0,8},{8,16},{16,24},{1,9},{9,17},{17,25},{2,10},{10,18},{18,26},{... | collective-permute-start | bytes 3145736 | tf_op jit(solution)/shard_map/ppermute | solution.py:386
  36.3 16.5 %copy-start = (bf16[3,3,256,256]{3,2,1,0:T(8,128)(2,1)S(1)}, bf16[3,3,256,256]{3,2,1,0:T(8,128)(2,1)}, u32[]{:S(2)}) copy-start(bf16[3,3,256,256]{3,2,1,0:T(8,128)(2,1)} %param.7) | copy-start | bytes 3538948
  36.3 2.4 %copy-start.2 = (bf16[3,3,512,512]{3,2,1,0:T(8,128)(2,1)S(1)}, bf16[3,3,512,512]{3,2,1,0:T(8,128)(2,1)}, u32[]{:S(2)}) copy-start(bf16[3,3,512,512]{3,2,1,0:T(8,128)(2,1)} %param.5) | copy-start | bytes 14155780
  48.7 30.1 %collective-permute-start.5 = (bf16[2,2,128,512]{3,2,1,0:T(8,128)(2,1)S(1)}, bf16[2,2,128,512]{3,2,1,0:T(8,128)(2,1)S(1)}, u32[]{:S(2)}, u32[]{:S(2)}) collective-permute-start(bf16[2,2,128,512]{3,2,1,0:T(8,128)(2,1)S(1)} %get-tuple-element.25.refs_6_.own_ref), channel_id=1, source_target_pairs={{0,8},{8,16},{16,24},{1,9},{9,17},{17,25},{2,10},{10,18},{18,26},{... | collective-permute-start | bytes 1572872 | tf_op jit(solution)/shard_map/ppermute | solution.py:386
  50.6 45.1 %collective-permute-start.9 = (bf16[3,2,128,512]{3,2,1,0:T(8,128)(2,1)S(1)}, bf16[3,2,128,512]{3,2,1,0:T(8,128)(2,1)S(1)}, u32[]{:S(2)}, u32[]{:S(2)}) collective-permute-start(bf16[3,2,128,512]{3,2,1,0:T(8,128)(2,1)S(1)} %get-tuple-element.30.refs_5_), channel_id=1, source_target_pairs={{0,8},{8,16},{16,24},{1,9},{9,17},{17,25},{2,10},{10,18},{18,26},{... | collective-permute-start | bytes 2359304 | tf_op jit(solution)/shard_map/ppermute | solution.py:386
  79.9 8.5 %collective-permute-start.7 = (bf16[1,4,128,256]{3,2,1,0:T(8,128)(2,1)S(1)}, bf16[1,4,128,256]{3,2,1,0:T(8,128)(2,1)S(1)}, u32[]{:S(2)}, u32[]{:S(2)}) collective-permute-start(bf16[1,4,128,256]{3,2,1,0:T(8,128)(2,1)S(1)} %get-tuple-element.38), channel_id=1, source_target_pairs={{0,1},{1,2},{2,3},{3,4},{4,5},{5,6},{6,7},{8,9},{9,10},{10,11},{11... | collective-permute-start | bytes 786440 | tf_op jit(solution)/shard_map/ppermute | solution.py:386
  81.8 7.5 %collective-permute-start.8 = (bf16[1,4,128,256]{3,2,1,0:T(8,128)(2,1)S(1)}, bf16[1,4,128,256]{3,2,1,0:T(8,128)(2,1)S(1)}, u32[]{:S(2)}, u32[]{:S(2)}) collective-permute-start(bf16[1,4,128,256]{3,2,1,0:T(8,128)(2,1)S(1)} %get-tuple-element.37), channel_id=1, source_target_pairs={{1,0},{2,1},{3,2},{4,3},{5,4},{6,5},{7,6},{9,8},{10,9},{11,10},{12... | collective-permute-start | bytes 786440 | tf_op jit(solution)/shard_map/ppermute | solution.py:391
  85.5 14.9 %collective-permute-start.3 = (bf16[1,2,128,512]{3,2,1,0:T(8,128)(2,1)S(1)}, bf16[1,2,128,512]{3,2,1,0:T(8,128)(2,1)S(1)}, u32[]{:S(2)}, u32[]{:S(2)}) collective-permute-start(bf16[1,2,128,512]{3,2,1,0:T(8,128)(2,1)S(1)} %get-tuple-element.24.refs_6_), channel_id=1, source_target_pairs={{0,8},{8,16},{16,24},{1,9},{9,17},{17,25},{2,10},{10,18},{18,26},{... | collective-permute-start | bytes 786440 | tf_op jit(solution)/shard_map/ppermute | solution.py:386

commit v3 on v2

--- a/solution.py
+++ b/solution.py
@@ -314,6 +314,7 @@
     count, frames, width, channels = x_ref.shape
     depth = pair_ref.shape[3]
     before, latest = [pair_ref[:, frame].reshape(count * width, depth) for frame in range(2)]
+    copies = []
     for pair in range(2):
         total = own_ref[plan["own_at"] : plan["own_at"] + count, pair].reshape(count * width, 2 * channels)
         if pair == 0:
@@ -328,25 +329,31 @@
             )
             for row in range(count):
                 activate(x_ref, act_ref, row, 2 * pair + half)
-    copies = []
-    for later, index, part, residual, taps in plan["terms"]:
-        total = None
-        for tap, row in taps:
-            lhs = act_ref[row].reshape(frames * width, 3 * channels)
-            value = jnp.dot(lhs, w_ref[tap], preferred_element_type=jnp.float32)
-            total = value if total is None else total + value
-        total = total.reshape(frames, width, channels)
-        if part is not None:
-            total += part_ref[part]
-        if residual is not None:
-            total += x_ref[residual].astype(jnp.float32)
-        if later:
-            later_ref[index] = total
+        if pair == 0 and count > 1:
             continue
-        place = len(copies)
-        stage_ref[place] = total.astype(jnp.bfloat16)
-        copies.append(pltpu.make_async_copy(stage_ref.at[place], out_ref.at[:, index], sem.at[place]))
-        copies[-1].start()
+        both = slice(2 * pair, 2 * pair + 2) if count == 1 else slice(0, frames)
+        wide = both.stop - both.start
+        place = 0
+        for later, index, part, residual, taps in plan["terms"]:
+            total = None
+            for tap, row in taps:
+                lhs = act_ref[row, both].reshape(wide * width, 3 * channels)
+                value = jnp.dot(lhs, w_ref[tap], preferred_element_type=jnp.float32)
+                total = value if total is None else total + value
+            total = total.reshape(wide, width, channels)
+            if part is not None:
+                total += part_ref[part, both]
+            if residual is not None:
+                total += x_ref[residual, both].astype(jnp.float32)
+            if later:
+                later_ref[index, both] = total
+                continue
+            stage_ref[place, both] = total.astype(jnp.bfloat16)
+            copies.append(
+                pltpu.make_async_copy(stage_ref.at[place, both], out_ref.at[both, index], sem.at[len(copies)])
+            )
+            copies[-1].start()
+            place += 1
     for copy in copies:
         copy.wait()
 
@@ -368,7 +375,7 @@
             pltpu.VMEM((count, frames, width, channels), jnp.bfloat16),
             pltpu.VMEM((count, frames, width, 3 * channels), jnp.bfloat16),
             pltpu.VMEM((final, frames, width, channels), jnp.bfloat16),
-            pltpu.SemaphoreType.DMA((final,)),
+            pltpu.SemaphoreType.DMA((2 * final,)),
         ],
         input_output_aliases={5: 0},
         compiler_params=pltpu.CompilerParams(vmem_limit_bytes=16 * MIB),

time: 103 us -> 103 us (level)
  no operation moved by 1% of the time
where the time goes in v3:
time: 103 us; the launch traced here: 102 us
  Pallas kernels  56.2 us (55%)
  starting transfers between devices  25.5 us (25%)
  waiting for transfers between devices  15.1 us (15%)
  local copies, waits for them, and re-layouts  5.24 us (5%)
    pallas_call x7, Pallas kernels, stage(): pl.pallas_call(functools.partial(stage_kernel, plan), out_shape=[jax.Shap...  50.4 us
    ppermute x8, starting transfers between devices, to_next(): return lax.ppermute(value, axis, [(i, i + 1) for i in range(count - 1)])  18.2 us
    ppermute x8, waiting for transfers between devices, to_next(): return lax.ppermute(value, axis, [(i, i + 1) for i in range(count - 1)])  14.1 us
    ppermute x2, starting transfers between devices, to_previous(): return lax.ppermute(value, axis, [(i + 1, i) for i in range(count - 1)])  7.29 us
    pallas_call x2, Pallas kernels, arrive(): pl.pallas_call(functools.partial(arrive_kernel, dict(terms=terms, own_at=...  4.79 us
    reshape x1, local copies, waits for them, and re-layouts, on_device(): time = time_weight.reshape(3, channels, 2 * depth)  2.77 us
    unnamed x6, local copies, waits for them, and re-layouts  2.43 us
  transfers between devices with their start and end apart: 10, of which 5 were waited for; matrix products, arithmetic and copies ran while one was open for 3% of the time, Pallas kernels for 48%

profile of v3, /device:TPU:20, one launch (start us, length us, event | category | flops | bytes accessed | tf_op | source)
XLA Modules:
  0.0 102.5 jit_solution(4373598797410986689)
XLA Ops:
  0.0 0.0 copy-start.1
  0.0 5.2 %hidden_1_2.1.refs_2_.refs_0_ = bf16[2,2,128,512]{3,2,1,0:T(8,128)(2,1)S(1)} custom-call(bf16[2,16,128,512]{3,2,1,0:T(8,128)(2,1)} %refs_0_.7, bf16[3,1536,512]{2,1,0:T(8,128)(2,1)} %bitcast.7), custom_call_target="tpu_custom_call" | custom-call | flops 2415919104 | bytes 1024 | tf_op jit(solution)/shard_map/hidden_1_2/pallas_call | solution.py:293
  5.2 3.4 %collective-permute-start.2 = (bf16[2,2,128,512]{3,2,1,0:T(8,128)(2,1)S(1)}, bf16[2,2,128,512]{3,2,1,0:T(8,128)(2,1)}, u32[]{:S(2)}, u32[]{:S(2)}) collective-permute-start(bf16[2,2,128,512]{3,2,1,0:T(8,128)(2,1)S(1)} %hidden_1_2.1.refs_2_.refs_0_), channel_id=1, source_target_pairs={{0,8},{8,16},{16,24},{1,9},{9,17},{17,25},{2,10},{10,18},{18,26},{... | collective-permute-start | bytes 1572872 | tf_op jit(solution)/shard_map/ppermute | solution.py:393
  8.6 0.0 copy-done.1
  8.6 7.1 %hidden_3_6.1.refs_2_ = bf16[4,2,128,512]{3,2,1,0:T(8,128)(2,1)S(1)} custom-call(bf16[2,16,128,512]{3,2,1,0:T(8,128)(2,1)} %refs_0_.7, bf16[3,1536,512]{2,1,0:T(8,128)(2,1)S(1)} %bitcast.8, bf16[2,2,128,512]{3,2,1,0:T(8,128)(2,1)S(1)} %hidden_1_2.1.refs_2_.refs_0_), custom_call_target="tpu_custom_call" | custom-call | flops 4831838208 | bytes 1024 | tf_op jit(solution)/shard_map/hidden_3_6/pallas_call | solution.py:293
  15.7 1.9 %collective-permute-start.4 = (bf16[4,2,128,512]{3,2,1,0:T(8,128)(2,1)S(1)}, bf16[4,2,128,512]{3,2,1,0:T(8,128)(2,1)}, u32[]{:S(2)}, u32[]{:S(2)}) collective-permute-start(bf16[4,2,128,512]{3,2,1,0:T(8,128)(2,1)S(1)} %hidden_3_6.1.refs_2_), channel_id=1, source_target_pairs={{0,8},{8,16},{16,24},{1,9},{9,17},{17,25},{2,10},{10,18},{18,26},{... | collective-permute-start | bytes 3145736 | tf_op jit(solution)/shard_map/ppermute | solution.py:393
  17.6 8.2 %hidden_7_10.1 = (bf16[4,2,128,512]{3,2,1,0:T(8,128)(2,1)}, bf16[2,1,128,512]{3,2,1,0:T(8,128)(2,1)}, bf16[2,1,128,512]{3,2,1,0:T(8,128)(2,1)}) custom-call(bf16[2,16,128,512]{3,2,1,0:T(8,128)(2,1)} %refs_0_.7, bf16[3,1536,512]{2,1,0:T(8,128)(2,1)S(1)} %bitcast.9, bf16[4,2,128,512]{3,2,1,0:T(8,128)(2,1)S(1)} %hidden_3_6.1.refs_2_), custom_call_target="tpu_custom_call" | custom-call | flops 4831838208 | bytes 1024 | tf_op jit(solution)/shard_map/hidden_7_10/pallas_call | solution.py:293
  25.8 1.9 %collective-permute-start = (bf16[2,1,128,512]{3,2,1,0:T(8,128)(2,1)}, bf16[2,1,128,512]{3,2,1,0:T(8,128)(2,1)S(1)}, u32[]{:S(2)}, u32[]{:S(2)}) collective-permute-start(bf16[2,1,128,512]{3,2,1,0:T(8,128)(2,1)} %get-tuple-element.21), channel_id=1, source_target_pairs={{0,1},{1,2},{2,3},{3,4},{4,5},{5,6},{6,7},{8,9},{9,10},{10,11},{11... | collective-permute-start | bytes 786440 | tf_op jit(solution)/shard_map/ppermute | solution.py:393
  27.8 3.6 %collective-permute-start.1 = (bf16[2,1,128,512]{3,2,1,0:T(8,128)(2,1)}, bf16[2,1,128,512]{3,2,1,0:T(8,128)(2,1)}, u32[]{:S(2)}, u32[]{:S(2)}) collective-permute-start(bf16[2,1,128,512]{3,2,1,0:T(8,128)(2,1)} %get-tuple-element.22), channel_id=1, source_target_pairs={{1,0},{2,1},{3,2},{4,3},{5,4},{6,5},{7,6},{9,8},{10,9},{11,10},{12... | collective-permute-start | bytes 786440 | tf_op jit(solution)/shard_map/ppermute | solution.py:398
  31.4 2.1 %collective-permute-start.6 = (bf16[4,2,128,512]{3,2,1,0:T(8,128)(2,1)}, bf16[4,2,128,512]{3,2,1,0:T(8,128)(2,1)}, u32[]{:S(2)}, u32[]{:S(2)}) collective-permute-start(bf16[4,2,128,512]{3,2,1,0:T(8,128)(2,1)} %get-tuple-element.23.refs_4_.refs_0_), channel_id=1, source_target_pairs={{0,8},{8,16},{16,24},{1,9},{9,17},{17,25},{2,10},{10,18},{18,26},{... | collective-permute-start | bytes 3145736 | tf_op jit(solution)/shard_map/ppermute | solution.py:393
  33.5 2.8 %reshape.11.refs_5_.refs_4_.w_ref.refs_8_.refs_3_ = bf16[3,512,512]{2,1,0:T(8,128)(2,1)S(1)} reshape(bf16[3,512,2,256]{3,2,1,0:T(2,128)(2,1)} %param.6) | data formatting | bytes 3145728 | tf_op jit(solution)/shard_map/reshape | solution.py:405
  36.3 0.0 copy-start
  36.3 0.0 collective-permute-done.refs_1_
  36.3 0.0 collective-permute-done.1.refs_2_
  36.3 0.0 collective-permute-done.2.refs_5_.refs_1_
  36.3 0.0 copy-start.2
  36.4 2.4 %copy-done.2 = bf16[3,3,512,512]{3,2,1,0:T(8,128)(2,1)S(1)} copy-done((bf16[3,3,512,512]{3,2,1,0:T(8,128)(2,1)S(1)}, bf16[3,3,512,512]{3,2,1,0:T(8,128)(2,1)}, u32[]{:S(2)}) %copy-start.2) | copy-done | bytes 4718616
  38.8 9.9 %hidden_rest.1 = (bf16[2,2,128,512]{3,2,1,0:T(8,128)(2,1)S(1)}, bf16[3,2,128,512]{3,2,1,0:T(8,128)(2,1)S(1)}, bf16[1,2,128,512]{3,2,1,0:T(8,128)(2,1)S(1)}) custom-call(bf16[2,16,128,512]{3,2,1,0:T(8,128)(2,1)} %refs_0_.7, bf16[2,1,128,512]{3,2,1,0:T(8,128)(2,1)S(1)} %collective-permute-done.refs_1_, ...), custom_call_target="tpu_custom_call" | custom-call | flops 7247757312 | bytes 1024 | tf_op jit(solution)/shard_map/hidden_rest/pallas_call | solution.py:293
  48.7 1.9 %collective-permute-start.5 = (bf16[2,2,128,512]{3,2,1,0:T(8,128)(2,1)S(1)}, bf16[2,2,128,512]{3,2,1,0:T(8,128)(2,1)S(1)}, u32[]{:S(2)}, u32[]{:S(2)}) collective-permute-start(bf16[2,2,128,512]{3,2,1,0:T(8,128)(2,1)S(1)} %get-tuple-element.25.refs_6_.own_ref), channel_id=1, source_target_pairs={{0,8},{8,16},{16,24},{1,9},{9,17},{17,25},{2,10},{10,18},{18,26},{... | collective-permute-start | bytes 1572872 | tf_op jit(solution)/shard_map/ppermute | solution.py:393
  50.6 2.1 %collective-permute-start.9 = (bf16[3,2,128,512]{3,2,1,0:T(8,128)(2,1)S(1)}, bf16[3,2,128,512]{3,2,1,0:T(8,128)(2,1)S(1)}, u32[]{:S(2)}, u32[]{:S(2)}) collective-permute-start(bf16[3,2,128,512]{3,2,1,0:T(8,128)(2,1)S(1)} %get-tuple-element.30.refs_5_), channel_id=1, source_target_pairs={{0,8},{8,16},{16,24},{1,9},{9,17},{17,25},{2,10},{10,18},{18,26},{... | collective-permute-start | bytes 2359304 | tf_op jit(solution)/shard_map/ppermute | solution.py:393
  52.8 0.0 collective-permute-done.4.refs_3_
  52.8 0.0 copy-done
  52.8 8.4 %out_2_5.1 = (bf16[4,16,128,256]{3,2,1,0:T(8,128)(2,1)}, bf16[2,4,128,256]{3,2,1,0:T(8,128)(2,1)S(1)}, bf16[2,4,128,256]{3,2,1,0:T(8,128)(2,1)S(1)}) custom-call(bf16[2,2,128,512]{3,2,1,0:T(8,128)(2,1)S(1)} %hidden_1_2.1.refs_2_.refs_0_, bf16[2,2,128,512]{3,2,1,0:T(8,128)(2,1)} %collective-permute-done.2.refs_5_.refs_1_, ...), custom_call_target="tpu_custom_call" | custom-call | flops 4831838208 | bytes 1024 | tf_op jit(solution)/shard_map/out_2_5/pallas_call | solution.py:293
  61.2 6.5 %collective-permute-done.6.refs_1_ = bf16[4,2,128,512]{3,2,1,0:T(8,128)(2,1)} collective-permute-done((bf16[4,2,128,512]{3,2,1,0:T(8,128)(2,1)}, bf16[4,2,128,512]{3,2,1,0:T(8,128)(2,1)}, u32[]{:S(2)}, u32[]{:S(2)}) %collective-permute-start.6) | collective-permute-done | bytes 1048608 | tf_op jit(solution)/shard_map/ppermute | solution.py:393
  67.7 7.5 %out_6_9.1 = (bf16[4,16,128,256]{3,2,1,0:T(8,128)(2,1)}, bf16[2,4,128,256]{3,2,1,0:T(8,128)(2,1)S(1)}) custom-call(bf16[4,2,128,512]{3,2,1,0:T(8,128)(2,1)} %get-tuple-element.23.refs_4_.refs_0_, bf16[4,2,128,512]{3,2,1,0:T(8,128)(2,1)} %collective-permute-done.6.refs_1_, ...), custom_call_target="tpu_custom_call", output_to_operand_aliasing={{0}: (5, {})} | custom-call | flops 4026531840 | bytes 1024 | tf_op jit(solution)/shard_map/out_6_9/pallas_call | solution.py:293
  75.2 3.7 %collective-permute-done.5.prev_ref = bf16[2,2,128,512]{3,2,1,0:T(8,128)(2,1)S(1)} collective-permute-done((bf16[2,2,128,512]{3,2,1,0:T(8,128)(2,1)S(1)}, bf16[2,2,128,512]{3,2,1,0:T(8,128)(2,1)S(1)}, u32[]{:S(2)}, u32[]{:S(2)}) %collective-permute-start.5) | collective-permute-done | bytes 524320 | tf_op jit(solution)/shard_map/ppermute | solution.py:393
  78.9 1.0 up_edges.1.refs_1_
  79.9 1.9 %collective-permute-start.7 = (bf16[1,4,128,256]{3,2,1,0:T(8,128)(2,1)S(1)}, bf16[1,4,128,256]{3,2,1,0:T(8,128)(2,1)S(1)}, u32[]{:S(2)}, u32[]{:S(2)}) collective-permute-start(bf16[1,4,128,256]{3,2,1,0:T(8,128)(2,1)S(1)} %get-tuple-element.38), channel_id=1, source_target_pairs={{0,1},{1,2},{2,3},{3,4},{4,5},{5,6},{6,7},{8,9},{9,10},{10,11},{11... | collective-permute-start | bytes 786440 | tf_op jit(solution)/shard_map/ppermute | solution.py:393
  81.8 3.6 %collective-permute-start.8 = (bf16[1,4,128,256]{3,2,1,0:T(8,128)(2,1)S(1)}, bf16[1,4,128,256]{3,2,1,0:T(8,128)(2,1)S(1)}, u32[]{:S(2)}, u32[]{:S(2)}) collective-permute-start(bf16[1,4,128,256]{3,2,1,0:T(8,128)(2,1)S(1)} %get-tuple-element.37), channel_id=1, source_target_pairs={{1,0},{2,1},{3,2},{4,3},{5,4},{6,5},{7,6},{9,8},{10,9},{11,10},{12... | collective-permute-start | bytes 786440 | tf_op jit(solution)/shard_map/ppermute | solution.py:398
  85.5 2.9 %collective-permute-start.3 = (bf16[1,2,128,512]{3,2,1,0:T(8,128)(2,1)S(1)}, bf16[1,2,128,512]{3,2,1,0:T(8,128)(2,1)S(1)}, u32[]{:S(2)}, u32[]{:S(2)}) collective-permute-start(bf16[1,2,128,512]{3,2,1,0:T(8,128)(2,1)S(1)} %get-tuple-element.24.refs_6_), channel_id=1, source_target_pairs={{0,8},{8,16},{16,24},{1,9},{9,17},{17,25},{2,10},{10,18},{18,26},{... | collective-permute-start | bytes 786440 | tf_op jit(solution)/shard_map/ppermute | solution.py:393
  88.4 0.0 collective-permute-done.7.refs_2_
  88.4 0.9 collective-permute-done.8.refs_4_
  89.3 4.2 %out_0_1.1 = (bf16[4,16,128,256]{3,2,1,0:T(8,128)(2,1)}, f32[4,4,128,256]{3,2,1,0:T(8,128)S(1)}, f32[4,2,128,512]{3,2,1,0:T(8,128)S(1)}) custom-call(bf16[2,4,128,256]{3,2,1,0:T(8,128)(2,1)S(1)} %get-tuple-element.26.refs_0_, bf16[2,4,128,256]{3,2,1,0:T(8,128)(2,1)S(1)} %up_edges.1.refs_1_, ...), custom_call_target="tpu_custom_call", output_to_operand_aliasing={{0}: (9, {})} | custom-call | flops 1207959552 | bytes 1024 | tf_op jit(solution)/shard_map/out_0_1/pallas_call | solution.py:293
  93.5 2.2 %collective-permute-done.9.refs_0_ = bf16[3,2,128,512]{3,2,1,0:T(8,128)(2,1)S(1)} collective-permute-done((bf16[3,2,128,512]{3,2,1,0:T(8,128)(2,1)S(1)}, bf16[3,2,128,512]{3,2,1,0:T(8,128)(2,1)S(1)}, u32[]{:S(2)}, u32[]{:S(2)}) %collective-permute-start.9) | collective-permute-done | bytes 786464 | tf_op jit(solution)/shard_map/ppermute | solution.py:393
  95.7 2.9 %out_10_15.1 = (bf16[4,16,128,256]{3,2,1,0:T(8,128)(2,1)}, f32[3,4,128,256]{3,2,1,0:T(8,128)S(1)}) custom-call(bf16[3,2,128,512]{3,2,1,0:T(8,128)(2,1)S(1)} %collective-permute-done.9.refs_0_, f32[4,2,128,512]{3,2,1,0:T(8,128)S(1)} %get-tuple-element.32.refs_1_, f32[4,4,128,256]{3,2,1,0:T(8,128)S(1)} %get-tuple-element.33.refs_2_, ...), custom_call_target="tpu_custom_call", output_to_operand_aliasing={{0}: (5, {})} | custom-call | flops 2013265920 | bytes 1024 | tf_op jit(solution)/shard_map/out_10_15/pallas_call | solution.py:369
  98.6 1.8 %collective-permute-done.3.refs_0_ = bf16[1,2,128,512]{3,2,1,0:T(8,128)(2,1)S(1)} collective-permute-done((bf16[1,2,128,512]{3,2,1,0:T(8,128)(2,1)S(1)}, bf16[1,2,128,512]{3,2,1,0:T(8,128)(2,1)S(1)}, u32[]{:S(2)}, u32[]{:S(2)}) %collective-permute-start.3) | collective-permute-done | bytes 262176 | tf_op jit(solution)/shard_map/ppermute | solution.py:393
  100.3 1.9 %out_12_14.1 = bf16[4,16,128,256]{3,2,1,0:T(8,128)(2,1)} custom-call(bf16[1,2,128,512]{3,2,1,0:T(8,128)(2,1)S(1)} %collective-permute-done.3.refs_0_, f32[4,2,128,512]{3,2,1,0:T(8,128)S(1)} %get-tuple-element.32.refs_1_, f32[3,4,128,256]{3,2,1,0:T(8,128)S(1)} %get-tuple-element.35.refs_2_, ...), custom_call_target="tpu_custom_call", output_to_operand_aliasing={{}: (5, {})} | custom-call | flops 872415232 | bytes 1024 | tf_op jit(solution)/shard_map/out_12_14/pallas_call | solution.py:369
  (1 shorter events, 0.0 us)
Async XLA Ops:
  0.0 8.6 %copy-start.1 = (bf16[3,3,512,512]{3,2,1,0:T(8,128)(2,1)S(1)}, bf16[3,3,512,512]{3,2,1,0:T(8,128)(2,1)}, u32[]{:S(2)}) copy-start(bf16[3,3,512,512]{3,2,1,0:T(8,128)(2,1)} %param.5) | copy-start | bytes 14155780
  5.2 31.1 %collective-permute-start.2 = (bf16[2,2,128,512]{3,2,1,0:T(8,128)(2,1)S(1)}, bf16[2,2,128,512]{3,2,1,0:T(8,128)(2,1)}, u32[]{:S(2)}, u32[]{:S(2)}) collective-permute-start(bf16[2,2,128,512]{3,2,1,0:T(8,128)(2,1)S(1)} %hidden_1_2.1.refs_2_.refs_0_), channel_id=1, source_target_pairs={{0,8},{8,16},{16,24},{1,9},{9,17},{17,25},{2,10},{10,18},{18,26},{... | collective-permute-start | bytes 1572872 | tf_op jit(solution)/shard_map/ppermute | solution.py:393
  15.7 37.1 %collective-permute-start.4 = (bf16[4,2,128,512]{3,2,1,0:T(8,128)(2,1)S(1)}, bf16[4,2,128,512]{3,2,1,0:T(8,128)(2,1)}, u32[]{:S(2)}, u32[]{:S(2)}) collective-permute-start(bf16[4,2,128,512]{3,2,1,0:T(8,128)(2,1)S(1)} %hidden_3_6.1.refs_2_), channel_id=1, source_target_pairs={{0,8},{8,16},{16,24},{1,9},{9,17},{17,25},{2,10},{10,18},{18,26},{... | collective-permute-start | bytes 3145736 | tf_op jit(solution)/shard_map/ppermute | solution.py:393
  25.8 10.5 %collective-permute-start = (bf16[2,1,128,512]{3,2,1,0:T(8,128)(2,1)}, bf16[2,1,128,512]{3,2,1,0:T(8,128)(2,1)S(1)}, u32[]{:S(2)}, u32[]{:S(2)}) collective-permute-start(bf16[2,1,128,512]{3,2,1,0:T(8,128)(2,1)} %get-tuple-element.21), channel_id=1, source_target_pairs={{0,1},{1,2},{2,3},{3,4},{4,5},{5,6},{6,7},{8,9},{9,10},{10,11},{11... | collective-permute-start | bytes 786440 | tf_op jit(solution)/shard_map/ppermute | solution.py:393
  27.8 8.6 %collective-permute-start.1 = (bf16[2,1,128,512]{3,2,1,0:T(8,128)(2,1)}, bf16[2,1,128,512]{3,2,1,0:T(8,128)(2,1)}, u32[]{:S(2)}, u32[]{:S(2)}) collective-permute-start(bf16[2,1,128,512]{3,2,1,0:T(8,128)(2,1)} %get-tuple-element.22), channel_id=1, source_target_pairs={{1,0},{2,1},{3,2},{4,3},{5,4},{6,5},{7,6},{9,8},{10,9},{11,10},{12... | collective-permute-start | bytes 786440 | tf_op jit(solution)/shard_map/ppermute | solution.py:398
  31.4 36.3 %collective-permute-start.6 = (bf16[4,2,128,512]{3,2,1,0:T(8,128)(2,1)}, bf16[4,2,128,512]{3,2,1,0:T(8,128)(2,1)}, u32[]{:S(2)}, u32[]{:S(2)}) collective-permute-start(bf16[4,2,128,512]{3,2,1,0:T(8,128)(2,1)} %get-tuple-element.23.refs_4_.refs_0_), channel_id=1, source_target_pairs={{0,8},{8,16},{16,24},{1,9},{9,17},{17,25},{2,10},{10,18},{18,26},{... | collective-permute-start | bytes 3145736 | tf_op jit(solution)/shard_map/ppermute | solution.py:393
  36.3 16.5 %copy-start = (bf16[3,3,256,256]{3,2,1,0:T(8,128)(2,1)S(1)}, bf16[3,3,256,256]{3,2,1,0:T(8,128)(2,1)}, u32[]{:S(2)}) copy-start(bf16[3,3,256,256]{3,2,1,0:T(8,128)(2,1)} %param.7) | copy-start | bytes 3538948
  36.3 2.4 %copy-start.2 = (bf16[3,3,512,512]{3,2,1,0:T(8,128)(2,1)S(1)}, bf16[3,3,512,512]{3,2,1,0:T(8,128)(2,1)}, u32[]{:S(2)}) copy-start(bf16[3,3,512,512]{3,2,1,0:T(8,128)(2,1)} %param.5) | copy-start | bytes 14155780
  48.7 30.1 %collective-permute-start.5 = (bf16[2,2,128,512]{3,2,1,0:T(8,128)(2,1)S(1)}, bf16[2,2,128,512]{3,2,1,0:T(8,128)(2,1)S(1)}, u32[]{:S(2)}, u32[]{:S(2)}) collective-permute-start(bf16[2,2,128,512]{3,2,1,0:T(8,128)(2,1)S(1)} %get-tuple-element.25.refs_6_.own_ref), channel_id=1, source_target_pairs={{0,8},{8,16},{16,24},{1,9},{9,17},{17,25},{2,10},{10,18},{18,26},{... | collective-permute-start | bytes 1572872 | tf_op jit(solution)/shard_map/ppermute | solution.py:393
  50.6 45.1 %collective-permute-start.9 = (bf16[3,2,128,512]{3,2,1,0:T(8,128)(2,1)S(1)}, bf16[3,2,128,512]{3,2,1,0:T(8,128)(2,1)S(1)}, u32[]{:S(2)}, u32[]{:S(2)}) collective-permute-start(bf16[3,2,128,512]{3,2,1,0:T(8,128)(2,1)S(1)} %get-tuple-element.30.refs_5_), channel_id=1, source_target_pairs={{0,8},{8,16},{16,24},{1,9},{9,17},{17,25},{2,10},{10,18},{18,26},{... | collective-permute-start | bytes 2359304 | tf_op jit(solution)/shard_map/ppermute | solution.py:393
  79.9 8.5 %collective-permute-start.7 = (bf16[1,4,128,256]{3,2,1,0:T(8,128)(2,1)S(1)}, bf16[1,4,128,256]{3,2,1,0:T(8,128)(2,1)S(1)}, u32[]{:S(2)}, u32[]{:S(2)}) collective-permute-start(bf16[1,4,128,256]{3,2,1,0:T(8,128)(2,1)S(1)} %get-tuple-element.38), channel_id=1, source_target_pairs={{0,1},{1,2},{2,3},{3,4},{4,5},{5,6},{6,7},{8,9},{9,10},{10,11},{11... | collective-permute-start | bytes 786440 | tf_op jit(solution)/shard_map/ppermute | solution.py:393
  81.8 7.5 %collective-permute-start.8 = (bf16[1,4,128,256]{3,2,1,0:T(8,128)(2,1)S(1)}, bf16[1,4,128,256]{3,2,1,0:T(8,128)(2,1)S(1)}, u32[]{:S(2)}, u32[]{:S(2)}) collective-permute-start(bf16[1,4,128,256]{3,2,1,0:T(8,128)(2,1)S(1)} %get-tuple-element.37), channel_id=1, source_target_pairs={{1,0},{2,1},{3,2},{4,3},{5,4},{6,5},{7,6},{9,8},{10,9},{11,10},{12... | collective-permute-start | bytes 786440 | tf_op jit(solution)/shard_map/ppermute | solution.py:398
  85.5 14.9 %collective-permute-start.3 = (bf16[1,2,128,512]{3,2,1,0:T(8,128)(2,1)S(1)}, bf16[1,2,128,512]{3,2,1,0:T(8,128)(2,1)S(1)}, u32[]{:S(2)}, u32[]{:S(2)}) collective-permute-start(bf16[1,2,128,512]{3,2,1,0:T(8,128)(2,1)S(1)} %get-tuple-element.24.refs_6_), channel_id=1, source_target_pairs={{0,8},{8,16},{16,24},{1,9},{9,17},{17,25},{2,10},{10,18},{18,26},{... | collective-permute-start | bytes 786440 | tf_op jit(solution)/shard_map/ppermute | solution.py:393
